TPU v7x, 32 devices: a whole 2x2x4 slice. The times are simulated.
32 devices in a mesh: dp: 8 (over y, x, core), mp: 4 (over z).
Axes of the slice: x: 2, y: 2, z: 4, core: 2. Of those that a mesh axis runs over, the one named last changes fastest.
Arguments:
- tokens: int32 [8, 1024], P('dp'), may hold values from 0 to 31
- lengths: int32 [8], P('dp'), may hold values from 30 to 1024, as said below
- tile_owner: int32 [192], replicated, may hold values from 0 to 191, each once
- step_count: int32 [], replicated, may hold values from 2 to 20
- weight_tiles: float32 [192, 128, 512], P('dp', None, 'mp'), may hold values from -0.1875 to 0.1875
- tiles_first: float32 [192, 128, 512], P('dp', None, 'mp'), may hold values from -9.536743e-06 to 9.536743e-06
- tiles_second: float32 [192, 128, 512], P('dp', None, 'mp'), may hold values from 1.6590697e-12 to 6.6520795e-12
- stats_left: float32 [192, 128, 512], P('dp', None, 'mp'), as said below
- stats_right: float32 [192, 128, 512], P('dp', None, 'mp'), as said below
- basis_left: float32 [192, 128, 512], P('dp', None, 'mp'), as said below
- basis_right: float32 [192, 128, 512], P('dp', None, 'mp'), as said below
- embedding: float32 [32, 1024], replicated, may hold values from -6 to 6
- embedding_first: float32 [32, 1024], replicated, may hold values from -2.670288e-05 to 2.670288e-05
- embedding_second: float32 [32, 1024], replicated, may hold values from 3.7329067e-13 to 1.4971129e-12
- head_table: float32 [1025, 32], replicated, may hold values from -0.1875 to 0.1875
- head_first: float32 [1025, 32], replicated, may hold values from -2.670288e-05 to 2.670288e-05
- head_second: float32 [1025, 32], replicated, may hold values from 1.4931627e-11 to 5.9884514e-11
- vectors: float32 [5, 1024], replicated
- vectors_first: float32 [5, 1024], replicated, may hold values from -2.670288e-05 to 2.670288e-05
- vectors_second: float32 [5, 1024], replicated, may hold values from 1.4931627e-11 to 5.9884514e-11
- fc_bias: float32 [1, 4096], P(None, 'mp'), may hold values from -4 to 4
- fc_bias_first: float32 [1, 4096], P(None, 'mp'), may hold values from -2.670288e-05 to 2.670288e-05
- fc_bias_second: float32 [1, 4096], P(None, 'mp'), may hold values from 1.4931627e-11 to 5.9884514e-11
Outputs:
- loss: float32 [], replicated
- grad_norm: float32 [], replicated
- new_tiles: float32 [192, 128, 512], P('dp', None, 'mp')
- tiles_low: bfloat16 [192, 128, 512], P('dp', None, 'mp')
- new_tiles_first: float32 [192, 128, 512], P('dp', None, 'mp')
- new_tiles_second: float32 [192, 128, 512], P('dp', None, 'mp')
- new_stats_left: float32 [192, 128, 512], P('dp', None, 'mp')
- new_stats_right: float32 [192, 128, 512], P('dp', None, 'mp')
- new_basis_left: float32 [192, 128, 512], P('dp', None, 'mp')
- new_basis_right: float32 [192, 128, 512], P('dp', None, 'mp')
- new_embedding: float32 [32, 1024], replicated
- new_embedding_first: float32 [32, 1024], replicated
- new_embedding_second: float32 [32, 1024], replicated
- new_head: float32 [1025, 32], replicated
- new_head_first: float32 [1025, 32], replicated
- new_head_second: float32 [1025, 32], replicated
- new_vectors: float32 [5, 1024], replicated
- new_vectors_first: float32 [5, 1024], replicated
- new_vectors_second: float32 [5, 1024], replicated
- new_fc_bias: float32 [1, 4096], P(None, 'mp')
- new_fc_bias_first: float32 [1, 4096], P(None, 'mp')
- new_fc_bias_second: float32 [1, 4096], P(None, 'mp')
Inputs may be any that keep to these rules, and one draw needn't show every extreme that they name: `lengths`: the 1 proteins of one length bucket stand in consecutive rows; some protein has length 1024. `tile_owner`: A permutation. `stats_left`: each tile is symmetric positive definite. `stats_right`: each tile is symmetric positive definite. `basis_left`: each tile has orthonormal columns. `basis_right`: each tile has orthonormal columns.
All inputs are finite; a program needn't handle non-finite values.
Results may differ from a plain program's by a relative error of at most 0.0063.
The roundings to bfloat16 on the way count: a program that leaves them out, or rounds other values in their place, can miss the bound.
Values may be sent and summed in bfloat16 or wider, within the bound.
No kernel may reach another device: no remote copies, remote signals or barrier semaphores. Data moves between devices by JAX's collectives and lax.ppermute only.
A program may use at most 192 MiB of HBM per device.

v0:
```python
import functools
import math

import jax
import jax.numpy as jnp
import numpy as np
from jax import lax
from jax.experimental import pallas as pl
from jax.experimental.pallas import tpu as pltpu
from jax.sharding import PartitionSpec as P

D = 1024
H = 16
HD = 64
ROT = 32
BS = 128
HB = 64
ROWS = 256
WIDE = 128
MEGA = 1024 * 1024

NORM_EPS = 1e-05
CLIP_NORM = 0.02
RATE_TILES = 0.02
RATE_SMALL = 0.2
BETA_ONE = 0.9
BETA_TWO = 0.95
ADAM_EPS = 1e-08
WEIGHT_DECAY = 0.01
MASKED = -1e30
GELU_A = math.sqrt(2.0 / math.pi)
GELU_B = 0.044715

NN = (((1,), (0,)), ((), ()))
NT = (((1,), (1,)), ((), ()))
TN = (((0,), (0,)), ((), ()))
f32 = jnp.float32
bf16 = jnp.bfloat16
SMEM = pl.BlockSpec(memory_space=pltpu.SMEM)
VMEM = pl.BlockSpec(memory_space=pltpu.VMEM)
ANY = pl.BlockSpec(memory_space=pl.ANY)


def dot(a, b, dims=NN):
    return lax.dot_general(a, b, dims, preferred_element_type=f32)


def split2(a):
    high = a.astype(bf16)
    return high, (a - high.astype(f32)).astype(bf16)


def split3(a):
    high = a.astype(bf16)
    rest = a - high.astype(f32)
    middle = rest.astype(bf16)
    return high, middle, (rest - middle.astype(f32)).astype(bf16)


def dot3(a, b, dims):
    (axis_a,), (axis_b,) = dims[0]
    ah, al = split2(a)
    bh, bl = split2(b)
    return dot(
        jnp.concatenate([ah, ah, al], axis=axis_a),
        jnp.concatenate([bh, bl, bh], axis=axis_b),
        dims,
    )


def dot6(a, b, dims):
    (axis_a,), (axis_b,) = dims[0]
    ah, am, al = split3(a)
    bh, bm, bl = split3(b)
    return dot(
        jnp.concatenate([ah, ah, am, am, ah, al], axis=axis_a),
        jnp.concatenate([bh, bm, bh, bm, bl, bh], axis=axis_b),
        dims,
    )


def rows_times_low(a, low, dims):
    count = a.shape[0]
    parts = dot(jnp.concatenate(split3(a), axis=0), low, dims)
    return parts[:count] + (parts[count : 2 * count] + parts[2 * count :])


def lanes(shape):
    return lax.broadcasted_iota(jnp.int32, shape, len(shape) - 1)


def sublanes(shape):
    return lax.broadcasted_iota(jnp.int32, shape, len(shape) - 2)


def stats_of(values):
    centred = values - jnp.mean(values, axis=-1, keepdims=True)
    spread = jnp.mean(centred * centred, axis=-1, keepdims=True)
    scale = lax.rsqrt(spread + NORM_EPS)
    return centred * scale, scale


def norm_back(grad, normed, scale, gain):
    inner = grad * gain
    mean_one = jnp.mean(inner, axis=-1, keepdims=True)
    mean_two = jnp.mean(inner * normed, axis=-1, keepdims=True)
    return scale * (inner - mean_one - normed * mean_two)


def params(microseconds, megabytes=20):
    return dict(
        compiler_params=pltpu.CompilerParams(vmem_limit_bytes=megabytes * MEGA),
        cost_estimate=pl.CostEstimate(
            flops=int(microseconds * 1.1e9), bytes_accessed=int(microseconds * 1e6), transcendentals=0
        ),
    )


def swap_with(value, axis, mask):
    count = lax.axis_size(axis)
    return lax.ppermute(value, axis, [(i, i ^ mask) for i in range(count)])


def tree_sum(parts):
    while len(parts) > 1:
        parts = [parts[i] + parts[i + 1] for i in range(0, len(parts), 2)]
    return parts[0]


def gather_xor(value, axis):
    return [value] + [swap_with(value, axis, r) for r in range(1, lax.axis_size(axis))]


def gather_halves(mine):
    return [swap_with(mine, "mp", r) for r in range(1, lax.axis_size("mp"))]


def swap_pair(parts):
    return [swap_with(part, "dp", 1) for part in parts]


def butterfly(kept):
    bits = [1 << k for k in range(1, lax.axis_size("dp").bit_length() - 1)]
    half = (kept.shape[0] // 2 + 7) // 8 * 8
    pieces = [kept[:half], kept[half:]]
    for k in range(len(bits)):
        received = [
            swap_with(piece, "dp", order[k])
            for piece, order in zip(pieces, (bits, bits[1:] + bits[:1]))
        ]
        pieces = [piece + other for piece, other in zip(pieces, received)]
    return jnp.concatenate(pieces, axis=0)


def direct(kept):
    return tree_sum([kept] + [swap_with(kept, "dp", r) for r in range(2, lax.axis_size("dp"), 2)])


def deal(upper, value, keep_o, send_o):
    half = keep_o.shape[0]

    @pl.when(upper == 0)
    def _():
        keep_o[...] = value[:half]
        send_o[...] = value[half : 2 * half]

    @pl.when(upper == 1)
    def _():
        keep_o[...] = value[half : 2 * half]
        send_o[...] = value[:half]


def join(upper, mine, other, whole):
    half = mine.shape[0]

    @pl.when(upper == 0)
    def _():
        whole[:half] = mine[...]
        whole[half:] = other[...]

    @pl.when(upper == 1)
    def _():
        whole[:half] = other[...]
        whole[half:] = mine[...]


def layer_shapes(heads_local, ff_local):
    return ((D, 3 * heads_local * HD), (heads_local * HD, D), (D, ff_local), (ff_local, D))


def tile_places(shapes):
    places = []
    for which, (row_total, col_total) in enumerate(shapes):
        for i in range(row_total // BS):
            for k in range(col_total // BS):
                places.append((which, i, k))
    return places


def first_places(heads, ff_local):
    q_cols = 3 * heads * HD // BS
    rows, blocks = [], []
    for which, i, k in tile_places(layer_shapes(heads, ff_local)):
        used = which in (0, 2)
        rows.append(i if used else 0)
        blocks.append(k if which == 0 else q_cols + k if which == 2 else q_cols + ff_local // BS)
    return np.array(rows, np.int32), np.array(blocks, np.int32)


def first_kernel(owner, ints, row_of, block_of, tiles, embed, vec, natural_o, low_o, normed_o, keep_o, send_o, rows, acc):
    count = tiles.shape[0]
    begin = ints[0] * count

    def find(b, carry):
        slot = owner[b] - begin

        @pl.when((slot >= 0) & (slot < count))
        def _():
            natural_o[slot] = b

        return carry

    lax.fori_loop(0, owner.shape[0], find, 0)
    normed, _ = stats_of(embed[...])
    low = (normed * vec[0:1] + vec[1:2]).astype(bf16)
    normed_o[...] = low
    for i in range(D // BS):
        rows[i] = low[:, i * BS : (i + 1) * BS]
    acc[...] = jnp.zeros_like(acc)
    for s in range(count):
        low_o[s] = tiles[s].astype(bf16)
    products = [dot(rows[row_of[natural_o[s]]], low_o[s]) for s in range(count)]
    for s in range(count):
        acc[block_of[natural_o[s]]] += products[s]
    half = keep_o.shape[0]
    for upper, first, second in ((0, keep_o, send_o), (1, send_o, keep_o)):

        @pl.when((ints[0] & 1) == upper)
        def _():
            first[...] = acc[:half]
            second[...] = acc[half : 2 * half]


def first_tables(owner, ints, tiles, embedding, vectors, heads, ff_local):
    vocab = embedding.shape[0]
    row_of, block_of = first_places(heads, ff_local)
    blocks = int(block_of.max())
    o = jax.ShapeDtypeStruct
    return pl.pallas_call(
        first_kernel,
        in_specs=[SMEM] * 4 + [VMEM] * 3,
        out_specs=[SMEM] + [VMEM] * 4,
        out_shape=[
            o((tiles.shape[0],), jnp.int32),
            o(tiles.shape, bf16),
            o((vocab, D), bf16),
            o(((blocks + 1) // 2, vocab, BS), f32),
            o(((blocks + 1) // 2, vocab, BS), f32),
        ],
        scratch_shapes=[
            pltpu.VMEM((D // BS, vocab, BS), bf16),
            pltpu.VMEM((blocks + 1, vocab, BS), f32),
        ],
        name="first_tables",
        **params(4, 56),
    )(owner, ints, jnp.asarray(row_of), jnp.asarray(block_of), tiles, embedding, vectors)


def second_places(heads, ff_local):
    pairs, across = heads // 2, D // BS
    lefts, blocks = [], []
    for which, i, k in tile_places(layer_shapes(heads, ff_local)):
        lefts.append(i if which == 1 else pairs + i if which == 3 else 0)
        blocks.append(
            i * across + k if which == 1 else (pairs * across + k if which == 3 else pairs * across + across)
        )
    return np.array(lefts, np.int32), np.array(blocks, np.int32)


def segments_of(heads, dp_count):
    return heads // 2 * (D // BS) * HB // dp_count, 32 * (D // BS) // dp_count


def second_kernel(
    heads, dp_count, natural, ints, left_of, block_of, mine, other, bias, low,
    proj_o, upper_o, act_o, values_o, keep_o, send_o, total, lefts, acc,
):
    vocab = proj_o.shape[0]
    me = ints[0]
    count = low.shape[0]
    pairs = heads // 2
    q_cols = 3 * heads * HD // BS
    f_rows = upper_o.shape[1] // BS
    across = D // BS
    join(me & 1, mine, other, total)
    for j in range(q_cols):
        proj_o[:, j * BS : (j + 1) * BS] = total[j]
    upper = jnp.concatenate([total[q_cols + j] for j in range(f_rows)], axis=1)
    upper = upper + bias[...]
    upper_o[...] = upper
    act = 0.5 * upper * (1.0 + jnp.tanh(GELU_A * (upper + GELU_B * (upper * upper * upper))))
    act = act.astype(bf16).astype(f32)
    act_o[...] = act.astype(bf16)
    values = proj_o[:, 2 * heads * HD :]
    shape = (heads * vocab, heads * HD)
    values = jnp.concatenate([values] * heads, axis=0)
    values = jnp.where(sublanes(shape) // vocab == lanes(shape) // HD, values, 0.0)
    values_o[...] = values.astype(bf16)
    for i in range(pairs):
        lefts[i] = values[i * HB : (i + 1) * HB, i * BS : (i + 1) * BS].astype(bf16)
    for i in range(f_rows):
        lefts[pairs + i] = padded(act[:, i * BS : (i + 1) * BS]).astype(bf16)
    acc[...] = jnp.zeros_like(acc)
    products = [dot(lefts[left_of[natural[s]]], low[s]) for s in range(count)]
    for s in range(count):
        rows = pl.ds(pl.multiple_of(block_of[natural[s]] * HB, HB), HB)
        acc[rows] += products[s]
    rows_v, rows_f = segments_of(heads, dp_count)
    base = pairs * across * HB
    for odd, first, second in ((0, keep_o, send_o), (1, send_o, keep_o)):

        @pl.when((me & 1) == odd)
        def _():
            for e in range(dp_count):
                out = second if e & 1 else first
                start = pl.multiple_of(((me ^ e) >> 1) * (rows_v + rows_f), 8)
                out[pl.ds(start, rows_v)] = acc[e * rows_v : (e + 1) * rows_v]
                k, inside = e * rows_f // vocab, e * rows_f % vocab
                at = base + k * HB + inside
                out[pl.ds(pl.multiple_of(start + rows_v, 8), rows_f)] = acc[at : at + rows_f]


def second_tables(natural, ints, mine, other, fc_bias, low, vocab, heads, dp_count):
    ff_local = fc_bias.shape[1]
    left_of, block_of = second_places(heads, ff_local)
    o = jax.ShapeDtypeStruct
    return pl.pallas_call(
        functools.partial(second_kernel, heads, dp_count),
        in_specs=[SMEM] * 4 + [VMEM] * 4,
        out_specs=[VMEM] * 6,
        out_shape=[
            o((vocab, 3 * heads * HD), f32),
            o((vocab, ff_local), f32),
            o((vocab, ff_local), bf16),
            o((heads * vocab, heads * HD), bf16),
            o((dp_count // 2 * sum(segments_of(heads, dp_count)), BS), f32),
            o((dp_count // 2 * sum(segments_of(heads, dp_count)), BS), f32),
        ],
        scratch_shapes=[
            pltpu.VMEM((2 * mine.shape[0],) + mine.shape[1:], f32),
            pltpu.VMEM((heads // 2 + ff_local // BS, HB, BS), bf16),
            pltpu.VMEM(((int(block_of.max()) + 1) * HB, BS), f32),
        ],
        name="second_tables",
        **params(4),
    )(natural, ints, jnp.asarray(left_of), jnp.asarray(block_of), mine, other, fc_bias, low)


def pack_kernel(rows_v, *refs):
    *parts, out = refs
    at = 0
    for part in parts:
        out[at : at + rows_v] = part[:rows_v].astype(bf16)
        at += rows_v
    down = tree_sum([part[rows_v:] for part in parts])
    for piece in split3(down):
        out[at : at + down.shape[0]] = piece
        at += down.shape[0]


def pack_segments(heads, dp_count, parts):
    rows_v, rows_f = segments_of(heads, dp_count)
    return pl.pallas_call(
        functools.partial(pack_kernel, rows_v),
        in_specs=[VMEM] * len(parts),
        out_specs=VMEM,
        out_shape=jax.ShapeDtypeStruct((len(parts) * rows_v + 3 * rows_f, BS), bf16),
        name="pack_segments",
        **params(1),
    )(*parts)


def assemble_kernel(places, owner, tiles, *mats):
    for index, (which, i, k) in enumerate(places):
        mats[which][i * BS : (i + 1) * BS, k * BS : (k + 1) * BS] = tiles[owner[index]]


def assemble(owner, tiles, heads, ff_local):
    shapes = layer_shapes(heads, ff_local)
    return pl.pallas_call(
        functools.partial(assemble_kernel, tile_places(shapes)),
        in_specs=[SMEM, VMEM],
        out_specs=[VMEM] * 4,
        out_shape=[jax.ShapeDtypeStruct(shape, bf16) for shape in shapes],
        name="assemble",
        **params(5),
    )(owner, tiles)


def rotary_tables(seq_len):
    half = ROT // 2
    frequency = np.float32(10000.0) ** (
        np.float32(-2.0) * np.arange(half, dtype=np.float32) / np.float32(ROT)
    )
    angles = np.arange(seq_len, dtype=np.float32)[:, None] * frequency[None, :].astype(np.float32)
    cosine = np.cos(angles.astype(np.float64)).astype(np.float32)
    sine = np.sin(angles.astype(np.float64)).astype(np.float32)
    wide_cos = np.ones((seq_len, WIDE), np.float32)
    wide_sin = np.zeros((seq_len, WIDE), np.float32)
    wide_cos[:, :half], wide_cos[:, half:ROT] = cosine, cosine
    wide_sin[:, :half], wide_sin[:, half:ROT] = sine, sine
    return wide_cos, wide_sin, np.ascontiguousarray(cosine.T), np.ascontiguousarray(sine.T)


def turned(x):
    half = ROT // 2
    lane = lanes(x.shape)
    return jnp.where(
        lane < half,
        -pltpu.roll(x, WIDE - half, 1),
        jnp.where(lane < ROT, pltpu.roll(x, half, 1), 0.0),
    )


def head_lanes(table, index):
    begin = index // 2 * WIDE
    chunk = table[:, begin : begin + WIDE]
    if index % 2:
        chunk = pltpu.roll(chunk, HD, 1)
    return jnp.where(lanes(chunk.shape) < HD, chunk, 0.0)


def stack_parts(table):
    high, middle, rest = split3(table)
    return jnp.concatenate([high, middle, rest, jnp.zeros_like(high)], axis=0)


def attention_kernel(
    heads, pair, length, token_col, proj, cosine, sine, before, query_o, key_o, weight_o, low_o, hot, key_hot, queries, wide
):
    seq = token_col.shape[0]
    vocab = proj.shape[0]
    lane = lanes((seq, WIDE))
    hot[...] = jnp.where(lane % vocab == token_col[...], 1.0, 0.0).astype(bf16)
    for n in range(2):
        first = (2 * pair + n) * vocab
        key_hot[n] = jnp.where(lane == token_col[...] + first, 1.0, 0.0).astype(bf16)
    one = lanes((vocab, WIDE)) == HD
    ones = (lanes((vocab, WIDE)) > HD) & (lanes((vocab, WIDE)) < HD + 4)
    for which in range(2):
        for n in range(2):
            own = head_lanes(proj, which * heads + 2 * pair + n)
            other = turned(own)
            if which == 0:
                own = jnp.where(one, 1.0, own * 0.125)
                other = other * 0.125
            else:
                own = jnp.where(one | ones, 1.0, own)
            begin = (which * 2 + n) * 2 * WIDE
            wide[:, begin : begin + WIDE] = stack_parts(own)
            wide[:, begin + WIDE : begin + 2 * WIDE] = stack_parts(other)
    for i in range(seq // ROWS):
        span = slice(i * ROWS, (i + 1) * ROWS)
        part = hot[span]
        position = i * ROWS + sublanes((ROWS, WIDE))
        bias = jnp.where(position < length[0], 0.0, MASKED)
        cos, sin = cosine[span], sine[span]
        key_cos = jnp.where(lanes((ROWS, WIDE)) == HD, bias, cos)
        for h in range(2):
            both = dot(part, wide[:, h * 2 * WIDE : (h + 1) * 2 * WIDE])
            queries[h, span] = (both[:, :WIDE] * cos + both[:, WIDE:] * sin).astype(bf16)
            k = 2 + h
            both = dot(part, wide[:, k * 2 * WIDE : (k + 1) * 2 * WIDE])
            key_o[h, span] = (both[:, :WIDE] * key_cos + both[:, WIDE:] * sin).astype(bf16)
    allowed = lanes((ROWS, ROWS)) <= sublanes((ROWS, ROWS))
    small = lanes((ROWS, WIDE))
    halves = []
    for i in range(seq // ROWS):
        span = slice(i * ROWS, (i + 1) * ROWS)
        past = i * ROWS
        weights = before[span] if pair else jnp.zeros((ROWS, WIDE), f32)
        query = [queries[h, span] for h in range(2)]
        near = [dot(query[h], key_o[h, span], NT) for h in range(2)]
        if past:
            far = [dot(query[h], key_o[h, :past], NT) for h in range(2)]
        near = [jnp.where(allowed, x, MASKED) for x in near]
        top = [jnp.max(x, axis=-1, keepdims=True) for x in near]
        if past:
            top = [jnp.maximum(m, jnp.max(x, axis=-1, keepdims=True)) for m, x in zip(top, far)]
            far = [jnp.exp(x - m) for m, x in zip(top, far)]
        near = [jnp.exp(x - m) for m, x in zip(top, near)]
        total = [jnp.sum(x, axis=-1, keepdims=True) for x in near]
        if past:
            total = [a + jnp.sum(x, axis=-1, keepdims=True) for a, x in zip(total, far)]
        share = [1.0 / a for a in total]
        near = [(x * a).astype(bf16) for x, a in zip(near, share)]
        if past:
            far = [(x * a).astype(bf16) for x, a in zip(far, share)]
        for h in range(2):
            weights = weights + dot(near[h], key_hot[h, span])
            if past:
                weights = weights + dot(far[h], key_hot[h, :past])
        for h in range(2):
            minus = -(top[h] + jnp.log(total[h]))
            high = minus.astype(bf16).astype(f32)
            middle = (minus - high).astype(bf16).astype(f32)
            rest = minus - high - middle
            value = jnp.where(small == HD + 3, rest, query[h].astype(f32))
            value = jnp.where(small == HD + 2, middle, value)
            query_o[h, span] = jnp.where(small == HD + 1, high, value).astype(bf16)
        weight_o[span] = weights
        own = weights if pair % 2 == 0 else pltpu.roll(weights, HD, 1)
        own = jnp.where(small < HD, own, 0.0)
        if i < seq // ROWS // 2:
            halves.append(own)
        else:
            k = i - seq // ROWS // 2
            low_o[k * ROWS : (k + 1) * ROWS] = (halves[k] + pltpu.roll(own, HD, 1)).astype(bf16)


def attention(pair, length, token_col, proj, cosine, sine, before, heads):
    seq = token_col.shape[0]
    vocab = proj.shape[0]
    o = jax.ShapeDtypeStruct
    return pl.pallas_call(
        functools.partial(attention_kernel, heads, pair),
        in_specs=[SMEM] + [VMEM] * 5,
        out_specs=[VMEM] * 4,
        out_shape=[
            o((2, seq, WIDE), bf16),
            o((2, seq, WIDE), bf16),
            o((seq, WIDE), f32),
            o((seq // 2, WIDE), bf16),
        ],
        scratch_shapes=[
            pltpu.VMEM((seq, WIDE), bf16),
            pltpu.VMEM((2, seq, WIDE), bf16),
            pltpu.VMEM((2, seq, WIDE), bf16),
            pltpu.VMEM((WIDE, 8 * WIDE), bf16),
        ],
        name="attention",
        **params(6),
    )(length, token_col, proj, cosine, sine, before)


def attention_back_kernel(
    heads,
    pair,
    token_col,
    token_row,
    query,
    key,
    weight,
    weight_grad,
    cosine,
    sine,
    cosine_t,
    sine_t,
    table_o,
    hot,
    mixed,
    query_grad,
    key_grad,
):
    seq = token_col.shape[0]
    vocab = table_o.shape[0]
    half = ROT // 2
    lane = lanes((seq, WIDE))
    hot[...] = jnp.where(
        (lane == token_col[...]) | (lane == token_col[...] + vocab) | ((lane >= HD) & (lane < HD + 3)),
        1.0,
        0.0,
    ).astype(bf16)
    grads = weight_grad[...]
    if heads * vocab < WIDE:
        grads = jnp.concatenate([grads, jnp.zeros((seq, WIDE - heads * vocab), f32)], axis=1)
    both = weight[...] * grads
    for n, h in enumerate((2 * pair, 2 * pair + 1)):
        inside = (lane >= h * vocab) & (lane < (h + 1) * vocab)
        minus = -jnp.sum(jnp.where(inside, both, 0.0), axis=-1, keepdims=True)
        own = grads if h == 0 else pltpu.roll(grads, WIDE - h * vocab, 1)
        own = jnp.where(lane < vocab, own, 0.0)
        high, rest = split2(own)
        m_high = minus.astype(bf16).astype(f32)
        m_middle = (minus - m_high).astype(bf16).astype(f32)
        m_rest = minus - m_high - m_middle
        value = high.astype(f32) + pltpu.roll(rest.astype(f32), vocab, 1)
        value = jnp.where(lane == HD, m_high, value)
        value = jnp.where(lane == HD + 1, m_middle, value)
        value = jnp.where(lane == HD + 2, m_rest, value)
        mixed[n] = value.astype(bf16)
    allowed = lanes((ROWS, ROWS)) <= sublanes((ROWS, ROWS))
    key_grad[...] = jnp.zeros_like(key_grad)
    both = range(2)
    for i in range(seq // ROWS):
        span = slice(i * ROWS, (i + 1) * ROWS)
        past = i * ROWS
        part = [query[n, span] for n in both]
        near = [dot(part[n], key[n, span], NT) for n in both]
        slope = [dot(mixed[n, span], hot[span], NT) for n in both]
        if past:
            far = [dot(part[n], key[n, :past], NT) for n in both]
            far_slope = [dot(mixed[n, span], hot[:past], NT) for n in both]
        near = [jnp.where(allowed, jnp.exp(x), 0.0) for x in near]
        near = [(x * y).astype(bf16) for x, y in zip(near, slope)]
        if past:
            far = [(jnp.exp(x) * y).astype(bf16) for x, y in zip(far, far_slope)]
        grad = [dot(near[n], key[n, span]) for n in both]
        if past:
            grad = [grad[n] + dot(far[n], key[n, :past]) for n in both]
        for n in both:
            key_grad[n, :, span] += dot(part[n], near[n], TN)[:HD]
            if past:
                key_grad[n, :, :past] += dot(part[n], far[n], TN)[:HD]
        for n in both:
            x = grad[n] * 0.125
            query_grad[n, span] = (x * cosine[span] - turned(x) * sine[span]).astype(bf16)
    shape = (vocab, seq)
    token_hot = jnp.where(sublanes(shape) == token_row[...], 1.0, 0.0).astype(bf16)
    small = lanes((vocab, WIDE)) < HD
    cos_t, sin_t = cosine_t[...], sine_t[...]
    one = dot(token_hot, query_grad[0])
    two = pltpu.roll(dot(token_hot, query_grad[1]), HD, 1)
    table_o[:, :WIDE] = jnp.where(small, one, two)
    turned_keys = []
    for n in range(2):
        front, back = key_grad[n, :half], key_grad[n, half:ROT]
        turned_keys += [front * cos_t + back * sin_t, back * cos_t - front * sin_t, key_grad[n, ROT:]]
    keys = jnp.concatenate(turned_keys, axis=0).astype(bf16)
    table_o[:, WIDE:] = dot(token_hot, keys, NT)


def attention_back(
    pair, token_col, token_row, query, key, weight, weight_grad, cosine, sine, cosine_t, sine_t, heads
):
    seq = token_col.shape[0]
    vocab = weight_grad.shape[1] // heads
    full = lambda array: pl.BlockSpec(array.shape, lambda i: (0,) * array.ndim)
    two = full(query)
    return pl.pallas_call(
        functools.partial(attention_back_kernel, heads, pair),
        grid=(1,),
        in_specs=[full(token_col), full(token_row), two, two, full(weight), full(weight_grad)]
        + [full(table) for table in (cosine, sine, cosine_t, sine_t)],
        out_specs=pl.BlockSpec((vocab, 2 * WIDE), lambda i: (0, 0)),
        out_shape=jax.ShapeDtypeStruct((vocab, 2 * WIDE), f32),
        scratch_shapes=[
            pltpu.VMEM((seq, WIDE), bf16),
            pltpu.VMEM((2, seq, WIDE), bf16),
            pltpu.VMEM((2, seq, WIDE), bf16),
            pltpu.VMEM((2, HD, seq), f32),
        ],
        name="attention_back",
        **params(6),
    )(token_col, token_row, query, key, weight, weight_grad, cosine, sine, cosine_t, sine_t)


def loss_kernel(
    parts,
    members,
    heads,
    ints,
    floats,
    token_col,
    target_col,
    token_row,
    embed,
    head,
    vec,
    *refs,
):
    pairs = heads // 2
    weights, refs = refs[: pairs * parts], refs[pairs * parts :]
    pieces, refs = refs[:members], refs[members:]
    keep_o, send_o, grad_o, sums_o, mixing, low_weights, table, down = refs
    step = pl.program_id(0)
    me, length, member = ints[0], ints[1], ints[2]
    vocab = embed.shape[0]
    height = heads * vocab

    @pl.when(step == 0)
    def _():
        rows_v, rows_f = segments_of(heads, members)
        small_v = min(rows_v, HB)
        for r in range(members):
            owner = member ^ r
            piece = pieces[r]
            for place in range(parts):
                for u in range(rows_v // small_v):
                    row = owner * rows_v + u * small_v
                    block, inside = row // HB, row % HB
                    i, k = block // (D // BS), block % (D // BS)
                    at = place * rows_v + u * small_v
                    mixing[
                        me ^ place,
                        pl.ds(pl.multiple_of(i * HB + inside, 32), small_v),
                        pl.ds(pl.multiple_of(k * BS, BS), BS),
                    ] = piece[at : at + small_v]
            at = parts * rows_v
            one, two, three = (
                piece[at + n * rows_f : at + (n + 1) * rows_f].astype(f32) for n in range(3)
            )
            row = owner * rows_f
            down[
                pl.ds(pl.multiple_of(row % vocab, 8), rows_f),
                pl.ds(pl.multiple_of(row // vocab * BS, BS), BS),
            ] = one + (two + three)
        table[...] = stack_parts(embed[...] + (down[...] + vec[2:3]))
        sums_o[...] = jnp.zeros_like(sums_o)

    second = step >= pl.num_programs(0) // 2
    small = lanes((ROWS, WIDE)) < HD

    def weights_of(r):
        value = weights[r][...].astype(f32)
        turned_value = pltpu.roll(value, HD, 1)
        value = jnp.where(second, turned_value, value)
        if pairs == 1:
            return jnp.where(small, value, 0.0)
        other = weights[parts + r][...].astype(f32)
        other = jnp.where(second, other, pltpu.roll(other, HD, 1))
        return jnp.where(small, value, other)

    own = weights_of(0)
    low_weights[me] = own.astype(bf16)[:, :height]
    for r in range(1, parts):
        low_weights[me ^ r] = weights_of(r).astype(bf16)[:, :height]
    token = token_col[...]
    hot = jnp.where(lanes((ROWS, WIDE)) % vocab == token, 1.0, 0.0).astype(bf16)
    x = dot(hot, table[...])
    x = x + dot(
        jnp.concatenate([low_weights[g] for g in range(parts)], axis=1),
        jnp.concatenate([mixing[g] for g in range(parts)], axis=0),
    )
    normed, scale = stats_of(x)
    gain = vec[3:4]
    final = (normed * gain + vec[4:5]).astype(bf16)
    head_low = head[:, :D].astype(bf16)
    square = (vocab, vocab)
    bias_row = jnp.sum(
        jnp.where(lanes(square) == sublanes(square), head[:, D : D + 1], 0.0), axis=0, keepdims=True
    )
    logits = dot(final, head_low, NT) + bias_row
    shifted = logits - jnp.max(logits, axis=-1, keepdims=True)
    log_probs = shifted - jnp.log(jnp.sum(jnp.exp(shifted), axis=-1, keepdims=True))
    target = lanes((ROWS, vocab)) == target_col[...]
    position = step * ROWS + sublanes((ROWS, 1))
    slot_weight = jnp.where(position < length - 1, floats[0], 0.0)
    picked = jnp.sum(jnp.where(target, log_probs, 0.0), axis=-1, keepdims=True)
    loss = -jnp.sum(slot_weight * picked, keepdims=True)
    logit_grad = ((jnp.exp(log_probs) - jnp.where(target, 1.0, 0.0)) * slot_weight).astype(bf16)
    final_grad = dot(logit_grad, head_low)
    grad = norm_back(final_grad, normed, scale, gain)
    high = grad.astype(bf16)
    token_hot = jnp.where(sublanes((vocab, ROWS)) == token_row[...], 1.0, 0.0).astype(bf16)
    both = dot(jnp.concatenate([own.T.astype(bf16), token_hot], axis=0), high)
    sums_o[0:vocab] += both[WIDE:]
    sums_o[vocab : 2 * vocab] += dot(logit_grad, final, TN)
    base = 2 * vocab
    sums_o[base : base + 1] += jnp.sum(final_grad * normed, axis=0, keepdims=True)
    sums_o[base + 1 : base + 2] += jnp.sum(final_grad, axis=0, keepdims=True)
    bias_grad = jnp.sum(logit_grad.astype(f32), axis=0, keepdims=True)
    sums_o[base + 2 : base + 3, :vocab] += bias_grad
    lane = lanes((1, WIDE))
    count = jnp.where((step == 0) & (length >= 2), 1.0, 0.0)
    sums_o[base + 3 : base + 4, :WIDE] += jnp.where(
        lane == 0, loss, jnp.where(lane == 1, count, 0.0)
    )
    sums_o[base + 16 : base + 16 + height] += both[:height]
    grad_o[...] = dot(high, mixing[me], NT)

    @pl.when(step == pl.num_programs(0) - 1)
    def _():
        deal(member & 1, sums_o, keep_o, send_o)


def loss_rows(
    ints,
    floats,
    token_col,
    target_col,
    token_row,
    embedding,
    head,
    vectors,
    weights,
    pieces,
    heads,
):
    seq = token_col.shape[0]
    vocab = embedding.shape[0]
    parts = len(weights) // (heads // 2)
    height = heads * vocab
    blocks = seq // ROWS // 2
    col = pl.BlockSpec((ROWS, 1), lambda i: (i, 0))
    o = jax.ShapeDtypeStruct
    full = lambda array: pl.BlockSpec(array.shape, lambda i: (0,) * array.ndim)
    sums_shape = (2 * vocab + 16 + height, D)
    return pl.pallas_call(
        functools.partial(loss_kernel, parts, len(pieces), heads),
        grid=(seq // ROWS,),
        in_specs=[SMEM, SMEM, col, col, pl.BlockSpec((1, ROWS), lambda i: (0, i))]
        + [full(embedding), full(head), full(vectors)]
        + [pl.BlockSpec((ROWS, WIDE), lambda i: (i % blocks, 0))] * len(weights)
        + [full(pieces[0])] * len(pieces),
        out_specs=[
            pl.BlockSpec((sums_shape[0] // 2, D), lambda i: (0, 0)),
            pl.BlockSpec((sums_shape[0] // 2, D), lambda i: (0, 0)),
            pl.BlockSpec((ROWS, height), lambda i: (i, 0)),
        ],
        out_shape=[o((sums_shape[0] // 2, D), f32)] * 2 + [o((seq, height), f32)],
        scratch_shapes=[
            pltpu.VMEM(sums_shape, f32),
            pltpu.VMEM((parts, height, D), bf16),
            pltpu.VMEM((parts, ROWS, height), bf16),
            pltpu.VMEM((4 * vocab, D), bf16),
            pltpu.VMEM((vocab, D), f32),
        ],
        name="loss_rows",
        **params(12),
    )(
        ints,
        floats,
        token_col,
        target_col,
        token_row,
        embedding,
        head,
        vectors,
        *weights,
        *pieces,
    )


def padded(block):
    lacking = HB - block.shape[0]
    if lacking:
        block = jnp.concatenate([block, jnp.zeros((lacking, block.shape[1]), block.dtype)], axis=0)
    return block


def put_left(ref, index, block):
    ref[index] = jnp.concatenate([padded(block)] * 3, axis=0).astype(bf16)


def put_right(ref, index, block):
    ref[index] = jnp.concatenate(split3(padded(block)), axis=0)


def factors_kernel(
    heads,
    ints,
    mine,
    other,
    mat_q,
    mat_o,
    mat_u,
    mat_f,
    upper,
    normed,
    act,
    values,
    left_o,
    right_o,
    hidden_o,
    bias_o,
    small_o,
    sums,
):
    vocab = normed.shape[0]
    width = mat_u.shape[1]
    join(ints[0] & 1, mine, other, sums)
    small_o[...] = sums[: small_o.shape[0]]
    rows = sums[0:vocab]
    mixed = sums[2 * vocab + 16 :]
    act_grad = rows_times_low(rows, mat_f[...], NT)
    u = upper[...]
    tanh = jnp.tanh(GELU_A * (u + GELU_B * (u * u * u)))
    slope = 0.5 * (1.0 + tanh) + 0.5 * u * (1.0 - tanh * tanh) * (
        GELU_A * (1.0 + 3.0 * GELU_B * (u * u))
    )
    upper_grad = act_grad * slope
    bias_grad = jnp.sum(upper_grad, axis=0, keepdims=True)
    bias_o[...] = bias_grad
    value_grad = rows_times_low(mixed, mat_o[...], NT)
    shape = value_grad.shape
    value_grad = jnp.where(sublanes(shape) // vocab == lanes(shape) // HD, value_grad, 0.0)
    value_table = value_grad[:vocab]
    for h in range(1, heads):
        value_table = value_table + value_grad[h * vocab : (h + 1) * vocab]
    hidden_o[0:vocab] = rows_times_low(upper_grad, mat_u[...], NT) + rows_times_low(
        value_table, mat_q[:, 2 * heads * HD :], NT
    )
    low = normed[...].astype(f32)
    own = act[...].astype(f32)
    val = values[...].astype(f32)
    square = (
        jnp.sum(
            dot6(low, low, NT)
            * (dot6(value_table, value_table, NT) + dot6(upper_grad, upper_grad, NT)),
            keepdims=True,
        )
        + jnp.sum(dot6(own, own, NT) * dot6(rows, rows, NT), keepdims=True)
        + jnp.sum(dot6(val, val, NT) * dot6(mixed, mixed, NT), keepdims=True)
        + jnp.sum(bias_grad * bias_grad, keepdims=True)
    )
    hidden_o[vocab : vocab + 16] = jnp.broadcast_to(square, (16, D))
    across = D // BS
    f_rows = width // BS
    pair = 2 * vocab
    for i in range(across):
        put_left(left_o, i, low[:, i * BS : (i + 1) * BS])
    for i in range(f_rows):
        put_left(left_o, across + i, own[:, i * BS : (i + 1) * BS])
    for i in range(heads // 2):
        put_left(
            left_o,
            across + f_rows + i,
            val[i * pair : (i + 1) * pair, i * BS : (i + 1) * BS],
        )
    at = 0
    for k in range(heads * HD // BS):
        put_right(right_o, at, value_table[:, k * BS : (k + 1) * BS])
        at += 1
    for i in range(heads // 2):
        for k in range(across):
            put_right(right_o, at, mixed[i * pair : (i + 1) * pair, k * BS : (k + 1) * BS])
            at += 1
    for k in range(f_rows):
        put_right(right_o, at, upper_grad[:, k * BS : (k + 1) * BS])
        at += 1
    for k in range(across):
        put_right(right_o, at, rows[:, k * BS : (k + 1) * BS])
        at += 1


def rest_kernel(pairs, ints, mine, other, hidden, mat_q, normed, right_o, hidden_o, half_o, table):
    vocab = normed.shape[0]
    join(ints[0] & 1, mine, other, table)
    blocks = [table[p * vocab : (p + 1) * vocab, :WIDE] for p in range(pairs)]
    blocks += [table[p * vocab : (p + 1) * vocab, WIDE:] for p in range(pairs)]
    grad = jnp.concatenate(blocks, axis=1)
    for k, block in enumerate(blocks):
        put_right(right_o, k, block)
    low = normed[...].astype(f32)
    square = jnp.sum(dot6(low, low, NT) * dot6(grad, grad, NT), keepdims=True)
    hidden_o[0:vocab] = hidden[0:vocab] + rows_times_low(grad, mat_q[:, : 2 * pairs * WIDE], NT)
    hidden_o[vocab:] = hidden[vocab:] + square
    size = half_o.shape[0]
    half_o[...] = hidden_o[pl.ds(pl.multiple_of((ints[0] & 1) * size, size), size)]


def factor_places(heads, ff_local):
    q_cols = 3 * heads * HD // BS
    o_rows = heads // 2
    across = D // BS
    f_rows = ff_local // BS
    left, right = [], []
    for which, i, k in tile_places(layer_shapes(heads, ff_local)):
        if which == 0:
            left.append(i)
            right.append(k)
        elif which == 1:
            left.append(across + f_rows + i)
            right.append(q_cols + i * across + k)
        elif which == 2:
            left.append(i)
            right.append(q_cols + o_rows * across + k)
        else:
            left.append(across + i)
            right.append(q_cols + o_rows * across + f_rows + k)
    return np.array(left, np.int32), np.array(right, np.int32)


def factors(ints, mine, other, mats, upper, normed, act, values, heads):
    vocab = normed.shape[0]
    ff_local = upper.shape[1]
    n_left = D // BS + ff_local // BS + heads // 2
    n_right = heads * HD // BS + heads // 2 * (D // BS) + ff_local // BS + D // BS
    o = jax.ShapeDtypeStruct
    return pl.pallas_call(
        functools.partial(factors_kernel, heads),
        in_specs=[SMEM] + [VMEM] * 10,
        out_specs=[VMEM] * 5,
        out_shape=[
            o((n_left, 3 * HB, BS), bf16),
            o((n_right, 3 * HB, BS), bf16),
            o((vocab + 16, D), f32),
            o((1, ff_local), f32),
            o((2 * vocab + 16, D), f32),
        ],
        scratch_shapes=[pltpu.VMEM((2 * mine.shape[0], D), f32)],
        name="factors",
        **params(7),
    )(ints, mine, other, *mats, upper, normed, act, values)


def factors_rest(ints, mine, other, hidden, mat_q, normed, heads):
    o = jax.ShapeDtypeStruct
    pairs = heads // 2
    return pl.pallas_call(
        functools.partial(rest_kernel, pairs),
        in_specs=[SMEM] + [VMEM] * 5,
        out_specs=[VMEM] * 3,
        out_shape=[
            o((2 * pairs, 3 * HB, BS), bf16),
            o(hidden.shape, f32),
            o((hidden.shape[0] // 2, D), f32),
        ],
        scratch_shapes=[pltpu.VMEM((2 * mine.shape[0], 2 * WIDE), f32)],
        name="factors_rest",
        **params(2),
    )(ints, mine, other, hidden, mat_q, normed)


def small_kernel(parts, corrections, ints, sums, own, *refs):
    mine, others, refs = refs[: parts - 1], refs[parts - 1 : 2 * parts - 2], refs[2 * parts - 2 :]
    bias_grad, refs = refs[0], refs[1:]
    weights, refs = refs[:12], refs[12:]
    outs, scalars, total = refs[:12], refs[12], refs[13]
    vocab = weights[0].shape[0]
    base = 2 * vocab
    size = own.shape[0] // 2
    for place, group in ((ints[0], mine), (1 - ints[0], others)):
        span = pl.ds(pl.multiple_of(place * size, size), size)
        total[span] = tree_sum([own[span]] + [ref[...] for ref in group])
    hidden = total[:vocab]
    square = total[vocab : vocab + 1, 0:1]
    rows = sums[0:vocab]
    normed, scale = stats_of(weights[0][...])
    gain = weights[6][0:1]
    embed_grad = rows + norm_back(hidden, normed, scale, gain)
    vector_grad = jnp.concatenate(
        [
            jnp.sum(hidden * normed, axis=0, keepdims=True),
            jnp.sum(hidden, axis=0, keepdims=True),
            jnp.sum(rows, axis=0, keepdims=True),
            sums[base : base + 1],
            sums[base + 1 : base + 2],
        ],
        axis=0,
    )
    head_grad = sums[vocab : 2 * vocab]
    head_bias = sums[base + 2 : base + 3, :vocab]
    add = lambda value: jnp.sum(value * value, keepdims=True)
    square = square + add(embed_grad) + add(vector_grad) + add(head_grad) + add(head_bias)
    count = sums[base + 3 : base + 4, 1:2]
    loss = sums[base + 3 : base + 4, 0:1] / count
    norm = jnp.sqrt(square) / count
    scale_all = jnp.minimum(1.0, CLIP_NORM / norm) / count
    one, two = corrections[0], corrections[1]

    def update(index, pick, grad):
        weight, first, second = (weights[3 * index + k][pick] for k in range(3))
        grad = grad * scale_all
        first = BETA_ONE * first + (1.0 - BETA_ONE) * grad
        second = BETA_TWO * second + (1.0 - BETA_TWO) * grad * grad
        step = first / one / (jnp.sqrt(second / two) + ADAM_EPS)
        outs[3 * index][pick] = weight - RATE_SMALL * (step + WEIGHT_DECAY * weight)
        outs[3 * index + 1][pick] = first
        outs[3 * index + 2][pick] = second

    everything = slice(None)
    update(0, everything, embed_grad)
    shape = (vocab, vocab)
    head_column = jnp.sum(
        jnp.where(lanes(shape) == sublanes(shape), head_bias, 0.0), axis=1, keepdims=True
    )
    update(1, (everything, slice(0, D)), head_grad)
    update(1, (everything, slice(D, D + 1)), head_column)
    update(2, everything, vector_grad)
    update(3, everything, bias_grad[...])
    lane = lanes((1, WIDE))
    scalars[...] = jnp.where(
        lane == 0, scale_all, jnp.where(lane == 1, loss, jnp.where(lane == 2, norm, 0.0))
    )


def small(corrections, upper, sums, hidden, mine, others, bias_grad, weights):
    o = jax.ShapeDtypeStruct
    return pl.pallas_call(
        functools.partial(small_kernel, 1 + len(mine)),
        in_specs=[SMEM] * 2 + [VMEM] * (2 + 2 * len(mine) + 1 + 12),
        out_specs=[VMEM] * 13,
        out_shape=[o(weight.shape, f32) for weight in weights] + [o((1, WIDE), f32)],
        scratch_shapes=[pltpu.VMEM(hidden.shape, f32)],
        name="small",
        **params(4),
    )(corrections, upper, sums, hidden, *mine, *others, bias_grad, *weights)


QB = 32
UNQ = 6
PER = 6


def take(value, at):
    return jnp.take_along_axis(value, at, axis=1, mode="promise_in_bounds")


def eliminate(packed, count):
    shape = (8, BS)
    lane, sub = lanes(shape), sublanes(shape)
    start = lane // QB * QB
    span = range(count)
    for p in range(QB // 8):
        r0 = 8 * p

        def body(step, carry):
            jj = 2 * step
            j = r0 + jj
            pick, pick_two = start + j, start + (j + 1)
            mark, mark_two = lane == pick, lane == pick_two
            below, below_two = sub > jj, sub > jj + 1
            wide = [jnp.broadcast_to(packed[t, pl.ds(j, 1), :], shape) for t in span]
            next_wide = [jnp.broadcast_to(packed[t, pl.ds(j + 1, 1), :], shape) for t in span]
            kept = [[packed[t, 8 * q : 8 * q + 8, :] for q in range(p, QB // 8)] for t in span]
            pivot = [take(w, pick) for w in wide]
            right = [take(w, pick_two) for w in wide]
            lower = [take(w, pick) for w in next_wide]
            corner = [take(w, pick_two) for w in next_wide]
            ones = [[take(a, pick) for a in group] for group in kept]
            twos = [[take(a, pick_two) for a in group] for group in kept]
            inverse = [1.0 / d for d in pivot]
            ratio = [b * i for b, i in zip(right, inverse)]
            inverse_two = [1.0 / (e - b * r) for e, b, r in zip(corner, lower, ratio)]
            scaled = [jnp.where(mark, 1.0, w) * i for w, i in zip(wide, inverse)]
            scaled_two = [
                jnp.where(mark_two, 1.0, jnp.where(mark, 0.0, w) - b * x) * i
                for w, b, x, i in zip(next_wide, lower, scaled, inverse_two)
            ]
            for t in span:
                for k, q in enumerate(range(p, QB // 8)):
                    a, c, d = kept[t][k], ones[t][k], twos[t][k]
                    d = d - c * ratio[t]
                    first = jnp.where(mark, 0.0, a) - c * scaled[t]
                    if k == 0:
                        first = jnp.where(below, first, a)
                    second = jnp.where(mark_two, 0.0, first) - d * scaled_two[t]
                    if k == 0:
                        second = jnp.where(below_two, second, first)
                    packed[t, 8 * q : 8 * q + 8, :] = second
            return carry

        lax.fori_loop(0, 4, body, 0)


def part_inverse(packed):
    shape = (QB, BS)
    lane, sub = lanes(shape), sublanes(shape)
    part, col = lane // QB, lane % QB
    diagonal = jnp.where(col == sub, packed, 0.0)
    pivot = jnp.ones(shape, f32)
    for k in range(BS // QB):
        own = jnp.sum(jnp.where(part == k, diagonal, 0.0), axis=1, keepdims=True)
        pivot = jnp.where(part == k, own, pivot)
    unit = jnp.where(col < sub, packed, jnp.where(col == sub, 1.0, 0.0))
    return unit * lax.rsqrt(pivot)


def inverse_factors(gram, packed, result, count):
    parts = BS // QB
    unroll = next(k for k in (UNQ, 3, 2, 1) if count % k == 0)
    lane32, sub32 = lanes((QB, BS)), sublanes((QB, BS))
    for b in range(parts):
        begin = b * QB
        below = begin + QB
        rows = slice(begin, below)
        here = lane32 // QB == b

        def pack(i, carry):
            for t in [i * unroll + k for k in range(unroll)]:
                value = jnp.zeros((QB, BS), f32)
                for k in range(parts):
                    block = gram[parts * t + k, rows, :]
                    if k != b:
                        block = pltpu.roll(block, (k * QB + BS - begin) % BS, 1)
                    value = jnp.where(lane32 // QB == k, block, value)
                packed[t] = value
            return carry

        lax.fori_loop(0, count // unroll, pack, 0)
        eliminate(packed, count)

        def spread(i, carry):
            groups = [i * unroll + k for k in range(unroll)]
            inverses = [part_inverse(packed[t]) for t in groups]
            firsts = [
                jnp.concatenate([jnp.where(lane32 // QB == k, x, 0.0) for k in range(parts)], axis=0)
                for x in inverses
            ]
            unit = jnp.where(lane32 - begin == sub32, 1.0, 0.0)
            panels = [
                jnp.concatenate(
                    [jnp.where(here, unit, gram[parts * t + k, rows, :]) for k in range(parts)],
                    axis=0,
                )
                for t in groups
            ]
            news = [dot6(x, y, NN) for x, y in zip(firsts, panels)]
            for t, new in zip(groups, news):
                for k in range(parts):
                    value = new[k * QB : (k + 1) * QB]
                    result[parts * t + k, rows, :] = (
                        jnp.where(lane32 < below, value, 0.0) if below < BS else value
                    )
            if below < BS:
                for t, new in zip(groups, news):
                    mats = [new[k * QB : (k + 1) * QB] for k in range(parts)]
                    changes = [dot6(x, x, TN) for x in mats]
                    shape = (BS - below, BS)
                    mark = lanes(shape) // QB == b
                    for k in range(parts):
                        old = gram[parts * t + k, below:, :]
                        gram[parts * t + k, below:, :] = jnp.where(mark, 0.0, old) - changes[k][below:]
            return carry

        lax.fori_loop(0, count // unroll, spread, 0)


def tile_params(count, per):
    blk = pl.BlockSpec((per, BS, BS), lambda i: (i, 0, 0))
    full = pl.BlockSpec((count, BS, BS), lambda i: (0, 0, 0))
    return blk, full, lambda dt: jax.ShapeDtypeStruct((count, BS, BS), dt)


def gradient_kernel(per, rest, natural, left_at, right_at, lefts, rights, more, L, R, QL, QR, *outs):
    step = pl.program_id(0)
    span = range(per)
    pairs = []
    for s in span:
        tile = natural[step * per + s]
        at = right_at[tile]
        right = jnp.where(
            at < rest, more[jnp.minimum(at, rest - 1)], rights[jnp.maximum(at - rest, 0)]
        )
        pairs.append((lefts[left_at[tile]], right))
    g = [dot(a, b, TN) for a, b in pairs]
    gt = [dot(b, a, TN) for a, b in pairs]
    qt = [QL[s].T for s in span]
    left = [dot3(x, x, NT) for x in g]
    right = [dot3(x, x, NT) for x in gt]
    rot = [dot3(q, x, NN) for q, x in zip(qt, g)]
    mixed_left = [dot3(left[s], QL[s], NN) for s in span]
    mixed_right = [dot3(right[s], QR[s], NN) for s in span]
    rot = [dot3(rot[s], QR[s], NN) for s in span]
    old_left = [dot6(L[s], QL[s], NN) for s in span]
    old_right = [dot6(R[s], QR[s], NN) for s in span]
    for s in span:
        for out, value in zip(
            outs, (left, right, rot, mixed_left, mixed_right, old_left, old_right)
        ):
            out[s] = value[s]


def gradient_products(natural, left_at, right_at, lefts, rights, more, L, R, QL, QR):
    count = QL.shape[0]
    blk, _, o = tile_params(count, PER)
    whole = lambda x: pl.BlockSpec(x.shape, lambda i: (0, 0, 0))
    return pl.pallas_call(
        functools.partial(gradient_kernel, PER, more.shape[0]),
        grid=(count // PER,),
        in_specs=[SMEM] * 3 + [whole(lefts), whole(rights), whole(more)] + [blk] * 4,
        out_specs=[blk] * 7,
        out_shape=[o(f32)] * 7,
        name="gradient_products",
        **params(9),
    )(natural, left_at, right_at, lefts, rights, more, L, R, QL, QR)


def soap_kernel(
    count, per, corrections, scal, GL, GR, GT, BL, BR, AL, AR, W, m, v, L, R, QL, QR,
    W_o, low_o, m_o, v_o, L_o, R_o, QL_o, QR_o, ML_s, MR_s, work, inv_s, packed,
):
    step = pl.program_id(0)
    scale = scal[0:1, 0:1]
    c1, c2 = corrections[0], corrections[1]
    span = range(per)
    share = (1 - BETA_TWO) * (scale * scale)
    xs = []
    for s in span:
        rot = GT[s] * scale
        mn = BETA_ONE * m[s] + (1 - BETA_ONE) * rot
        vn = BETA_TWO * v[s] + (1 - BETA_TWO) * rot * rot
        m_o[s] = mn
        v_o[s] = vn
        xs.append((mn / c1) / (jnp.sqrt(vn / c2) + ADAM_EPS))
    ML = [BETA_TWO * AL[s] + share * BL[s] for s in span]
    MR = [BETA_TWO * AR[s] + share * BR[s] for s in span]
    back = [dot3(QL[s], xs[s], NN) for s in span]
    ML = [x * lax.rsqrt(jnp.sum(x * x, keepdims=True)) for x in ML]
    MR = [x * lax.rsqrt(jnp.sum(x * x, keepdims=True)) for x in MR]
    back = [dot3(back[s], QR[s], NT) for s in span]
    gram_left = [dot6(x, x, TN) for x in ML]
    gram_right = [dot6(x, x, TN) for x in MR]
    for s in span:
        L_o[s] = BETA_TWO * L[s] + share * GL[s]
        R_o[s] = BETA_TWO * R[s] + share * GR[s]
        w = W[s]
        wn = w - RATE_TILES * (back[s] + WEIGHT_DECAY * w)
        W_o[s] = wn
        low_o[s] = wn.astype(bf16)
        t = step * per + s
        ML_s[t] = ML[s]
        MR_s[t] = MR[s]
        work[2 * t] = gram_left[s]
        work[2 * t + 1] = gram_right[s]

    @pl.when(step == pl.num_programs(0) - 1)
    def _():
        inverse_factors(work, packed, inv_s, count // 2)
        unroll = next(k for k in (8, 6, 3, 1) if count % k == 0)

        def last(i, carry):
            ts = [i * unroll + k for k in range(unroll)]
            ol = [dot3(ML_s[t], inv_s[2 * t], NT) for t in ts]
            orr = [dot3(MR_s[t], inv_s[2 * t + 1], NT) for t in ts]
            for t, a, b in zip(ts, ol, orr):
                QL_o[t] = a
                QR_o[t] = b
            return carry

        lax.fori_loop(0, count // unroll, last, 0)


def soap(corrections, scal, products, W, m, v, L, R, QL, QR):
    count = W.shape[0]
    blk, full, o = tile_params(count, PER)
    return pl.pallas_call(
        functools.partial(soap_kernel, count, PER),
        grid=(count // PER,),
        in_specs=[SMEM, pl.BlockSpec((1, WIDE), lambda i: (0, 0))] + [blk] * 14,
        out_specs=[blk] * 6 + [full] * 2,
        out_shape=[o(f32), o(bf16), o(f32), o(f32), o(f32), o(f32), o(f32), o(f32)],
        scratch_shapes=[pltpu.VMEM((count, BS, BS), f32)] * 2
        + [pltpu.VMEM((2 * count, BS, BS), f32)] * 2
        + [pltpu.VMEM((count // 2, QB, BS), f32)],
        name="soap_tiles",
        **params(40, 48),
    )(corrections, scal, *products, W, m, v, L, R, QL, QR)


def local(
    tokens,
    lengths,
    tile_owner,
    step_count,
    weight_tiles,
    tiles_first,
    tiles_second,
    stats_left,
    stats_right,
    basis_left,
    basis_right,
    embedding,
    embedding_first,
    embedding_second,
    head_table,
    head_first,
    head_second,
    vectors,
    vectors_first,
    vectors_second,
    fc_bias,
    fc_bias_first,
    fc_bias_second,
):
    seq = tokens.shape[1]
    mp_count = lax.axis_size("mp")
    dp_count = lax.axis_size("dp")
    dp_index = lax.axis_index("dp")
    mp_index = lax.axis_index("mp")
    upper_pair = dp_index & 1
    heads = H // mp_count
    ff_local = fc_bias.shape[1]
    count = weight_tiles.shape[0]
    vocab = embedding.shape[0]
    own_index = dp_index[None]

    natural, low_tiles, normed, keep, send = first_tables(
        tile_owner, own_index, weight_tiles, embedding, vectors, heads, ff_local
    )
    token_col = tokens.reshape(seq, 1)
    target_col = jnp.roll(tokens, -1, axis=1).reshape(seq, 1)
    keep = keep + swap_with(send, "dp", 1)
    mine = direct(keep)
    low_tiles, mine = lax.optimization_barrier((low_tiles, mine))
    gathered = lax.all_gather(low_tiles, "dp", axis=0, tiled=True)
    proj, upper, act, values, keep, send = second_tables(
        natural, own_index, mine, swap_with(mine, "dp", 1), fc_bias, low_tiles, vocab, heads, dp_count
    )
    cosine, sine, cosine_t, sine_t = rotary_tables(seq)
    segment = sum(segments_of(heads, dp_count))
    places = range(1, dp_count // 2)
    received = [swap_with(send, "dp", 1)]
    queries, keys = [], []
    weight = jnp.zeros((8, WIDE), f32)
    for pair in range(heads // 2):
        query, key, weight, weight_low = attention(
            pair, lengths, token_col, proj, cosine, sine, weight, heads
        )
        queries.append(query)
        keys.append(key)
        if pair == 0:
            received, weight, weight_low = lax.optimization_barrier((received, weight, weight_low))
            keep = keep + received[0]
            received = [
                swap_with(keep[q * segment : (q + 1) * segment], "dp", 2 * q) for q in places
            ]
            keep, weight = lax.optimization_barrier((keep, weight))
            weights = gather_xor(weight_low, "mp")
    if heads > 2:
        more = gather_xor(weight_low, "mp")
        received, weights, more[0] = lax.optimization_barrier((received, weights, more[0]))
    mine = tree_sum([keep[:segment]] + list(received))
    packed = pack_segments(heads, dp_count, gather_xor(mine, "mp"))
    even = [packed] + [swap_with(packed, "dp", 2 * q) for q in places]
    if heads > 2:
        even, more = lax.optimization_barrier((even, more))
        weights = weights + more
    odd = [swap_with(piece, "dp", 1) for piece in even]
    pieces = [piece for two in zip(even, odd) for piece in two]
    length = lengths[0]
    inverse_length = 1.0 / jnp.maximum(length - 1, 1).astype(f32)
    keep, send, weight_grad = loss_rows(
        jnp.stack([mp_index, length, dp_index]),
        inverse_length[None],
        token_col,
        target_col,
        tokens,
        embedding,
        head_table.T,
        vectors,
        weights,
        pieces,
        heads,
    )
    keep = keep + swap_with(send, "dp", 1)
    tables_back = []
    for pair in range(heads // 2):
        if pair == 1:
            weight_grad, keep = lax.optimization_barrier((weight_grad, keep))
        tables_back.append(
            attention_back(
                pair,
                token_col,
                tokens,
                queries[pair],
                keys[pair],
                weight,
                weight_grad,
                cosine,
                sine,
                cosine_t,
                sine_t,
                heads,
            )
        )
    mine = butterfly(keep)
    table = jnp.concatenate(tables_back, axis=0)
    half = table.shape[0] // 2
    first, second = table[:half], table[half:]
    is_upper = upper_pair == 1
    table = jnp.where(is_upper, second, first) + swap_with(
        jnp.where(is_upper, first, second), "dp", 1
    )
    gathered, table = lax.optimization_barrier((gathered, table))
    mats = assemble(tile_owner, gathered, heads, ff_local)
    table = direct(table)
    mine, mats = lax.optimization_barrier((mine, mats))
    left, right, hidden, bias_grad, sums = factors(
        own_index, mine, swap_with(mine, "dp", 1), mats, upper, normed, act, values, heads
    )
    more, hidden, hidden_half = factors_rest(
        own_index, table, swap_with(table, "dp", 1), hidden, mats[0], normed, heads
    )
    hidden_parts = gather_halves(hidden_half)
    left_at, right_at = (jnp.asarray(places) for places in factor_places(heads, ff_local))
    gradients = gradient_products(
        natural, left_at, right_at, left, right, more, stats_left, stats_right, basis_left, basis_right
    )
    hidden_parts, gradients = lax.optimization_barrier((hidden_parts, gradients))
    hidden_others = swap_pair(hidden_parts)
    corrections = 1.0 - jnp.power(
        jnp.array([BETA_ONE, BETA_TWO], f32), step_count.astype(f32)
    )
    small_weights = (
        embedding,
        embedding_first,
        embedding_second,
        head_table.T,
        head_first.T,
        head_second.T,
        vectors,
        vectors_first,
        vectors_second,
        fc_bias,
        fc_bias_first,
        fc_bias_second,
    )
    *small_out, scalars = small(
        corrections,
        upper_pair[None],
        sums,
        hidden,
        hidden_parts,
        hidden_others,
        bias_grad,
        small_weights,
    )
    small_out[3:6] = [value.T for value in small_out[3:6]]
    results = soap(
        corrections,
        scalars,
        gradients,
        weight_tiles,
        tiles_first,
        tiles_second,
        stats_left,
        stats_right,
        basis_left,
        basis_right,
    )
    return (scalars[0, 1], scalars[0, 2], *results, *small_out)


def solution(mesh):
    tiled = P("dp", None, "mp")
    split = P(None, "mp")
    in_specs = (P("dp", None), P("dp"), P(), P(), *[tiled] * 7, *[P()] * 9, *[split] * 3)
    out_specs = (P(), P(), *[tiled] * 8, *[P()] * 9, *[split] * 3)
    return jax.shard_map(local, mesh=mesh, in_specs=in_specs, out_specs=out_specs, check_vma=False)
```

profile of v0, /device:TPU:0, one launch (start us, length us, event | category | flops | bytes accessed | tf_op | source)
XLA Modules:
  0.0 218.9 jit_solution(16988578991666489376)
XLA Ops:
  7.2 5.2 %first_tables.1 = (s32[24]{0:T(128)}, bf16[24,128,128]{2,1,0:T(8,128)(2,1)}, bf16[32,1024]{1,0:T(8,128)(2,1)}, f32[7,32,128]{2,1,0:T(8,128)}, f32[7,32,128]{2,1,0:T(8,128)}) custom-call(s32[192]{0:T(256)} %owner.3, s32[1]{0:T(128)} %bitcast.1.ints, s32[192]{0:T(256)} %constant.45.clone.row_of, s32[192]{0:T(256)} %constant.46.clone.block_of, ...), custom_call_target="tpu_custom_call" | custom-call | flops 4400000000 | bytes 4000000 | tf_op jit(solution)/shard_map/first_tables/pallas_call | solution.py:249
  13.1 1.2 collective-permute-done
  15.2 2.9 %collective-permute-start.1 = (f32[7,32,128]{2,1,0:T(8,128)S(1)}, f32[7,32,128]{2,1,0:T(8,128)S(1)}, u32[]{:S(2)}, u32[]{:S(2)}) collective-permute-start(f32[7,32,128]{2,1,0:T(8,128)S(1)} %add.53), channel_id=1, source_target_pairs={{0,8},{4,12},{8,0},{12,4},{16,24},{20,28},{24,16},{28,20},{1,9},{5... | collective-permute-start | bytes 344072 | tf_op jit(solution)/shard_map/ppermute | solution.py:121
  18.1 1.5 collective-permute-start.2
  19.6 2.0 collective-permute-done.1
  21.6 3.9 %collective-permute-done.2 = f32[7,32,128]{2,1,0:T(8,128)S(1)} collective-permute-done((f32[7,32,128]{2,1,0:T(8,128)S(1)}, f32[7,32,128]{2,1,0:T(8,128)S(1)}, u32[]{:S(2)}, u32[]{:S(2)}) %collective-permute-start.2) | collective-permute-done | bytes 114720 | tf_op jit(solution)/shard_map/ppermute | solution.py:121
  27.0 1.1 second_tables.1
  28.9 4.1 %attention.2 = (bf16[2,1024,128]{2,1,0:T(8,128)(2,1)S(1)}, bf16[2,1024,128]{2,1,0:T(8,128)(2,1)S(1)}, f32[1024,128]{1,0:T(8,128)S(1)}, bf16[512,128]{1,0:T(8,128)(2,1)S(1)}) custom-call(s32[1]{0:T(128)S(6)} %copy.68.length, s32[1024,1]{1,0:T(8,128)S(1)} %copy.64.token_col, f32[32,768]{1,0:T(8,128)S(1)} %get-tuple-element.134.proj, ...), custom_call_target="tpu_custom_call" | custom-call | flops 6600000000 | bytes 6000000 | tf_op jit(solution)/shard_map/attention/pallas_call | solution.py:525
  33.1 1.3 collective-permute-start.6
  34.4 2.6 %collective-permute-start.10 = (bf16[512,128]{1,0:T(8,128)(2,1)S(1)}, bf16[512,128]{1,0:T(8,128)(2,1)S(1)}, u32[]{:S(2)}, u32[]{:S(2)}) collective-permute-start(bf16[512,128]{1,0:T(8,128)(2,1)S(1)} %get-tuple-element.142.refs_0_), channel_id=1, source_target_pairs={{0,2},{1,3},{2,0},{3,1},{4,6},{5,7},{6,4},{7,5},{8,10},{9,11},{10,... | collective-permute-start | bytes 393224 | tf_op jit(solution)/shard_map/ppermute | solution.py:121
  37.0 1.3 collective-permute-start.11
  39.6 1.5 collective-permute-start.8
  41.1 4.0 %attention.3 = (bf16[2,1024,128]{2,1,0:T(8,128)(2,1)S(1)}, bf16[2,1024,128]{2,1,0:T(8,128)(2,1)S(1)}, f32[1024,128]{1,0:T(8,128)S(1)}, bf16[512,128]{1,0:T(8,128)(2,1)S(1)}) custom-call(s32[1]{0:T(128)S(6)} %copy.68.length, s32[1024,1]{1,0:T(8,128)S(1)} %copy.64.token_col, f32[32,768]{1,0:T(8,128)S(1)} %get-tuple-element.134.proj, ...), custom_call_target="tpu_custom_call" | custom-call | flops 6600000000 | bytes 6000000 | tf_op jit(solution)/shard_map/attention/pallas_call | solution.py:525
  47.8 2.2 %collective-permute-start.12 = (f32[160,128]{1,0:T(8,128)S(1)}, f32[160,128]{1,0:T(8,128)S(1)}, u32[]{:S(2)}, u32[]{:S(2)}) collective-permute-start(f32[160,128]{1,0:T(8,128)S(1)} %add_add_fusion.1.refs_0_), channel_id=1, source_target_pairs={{0,1},{1,0},{2,3},{3,2},{4,5},{5,4},{6,7},{7,6},{8,9},{9,8},{10,11... | collective-permute-start | bytes 245768 | tf_op jit(solution)/shard_map/ppermute | solution.py:121
  50.0 2.0 collective-permute-start.13
  52.0 1.4 collective-permute-start.14
  54.0 2.4 %collective-permute-done.13.refs_2_ = f32[160,128]{1,0:T(8,128)S(1)} collective-permute-done((f32[160,128]{1,0:T(8,128)S(1)}, f32[160,128]{1,0:T(8,128)S(1)}, u32[]{:S(2)}, u32[]{:S(2)}) %collective-permute-start.13) | collective-permute-done | bytes 81952 | tf_op jit(solution)/shard_map/ppermute | solution.py:121
  56.3 3.9 %collective-permute-done.14.refs_3_ = f32[160,128]{1,0:T(8,128)S(1)} collective-permute-done((f32[160,128]{1,0:T(8,128)S(1)}, f32[160,128]{1,0:T(8,128)S(1)}, u32[]{:S(2)}, u32[]{:S(2)}) %collective-permute-start.14) | collective-permute-done | bytes 81952 | tf_op jit(solution)/shard_map/ppermute | solution.py:121
  61.1 1.5 collective-permute-start.16
  62.6 1.2 collective-permute-start.17
  63.8 2.4 %collective-permute-start.19 = (bf16[512,128]{1,0:T(8,128)(2,1)S(1)}, bf16[512,128]{1,0:T(8,128)(2,1)S(1)}, u32[]{:S(2)}, u32[]{:S(2)}) collective-permute-start(bf16[512,128]{1,0:T(8,128)(2,1)S(1)} %get-tuple-element.151.refs_4_), channel_id=1, source_target_pairs={{0,2},{1,3},{2,0},{3,1},{4,6},{5,7},{6,4},{7,5},{8,10},{9,11},{10,... | collective-permute-start | bytes 393224 | tf_op jit(solution)/shard_map/ppermute | solution.py:121
  68.4 6.9 %collective-permute-done.19.refs_6_ = bf16[512,128]{1,0:T(8,128)(2,1)S(1)} collective-permute-done((bf16[512,128]{1,0:T(8,128)(2,1)S(1)}, bf16[512,128]{1,0:T(8,128)(2,1)S(1)}, u32[]{:S(2)}, u32[]{:S(2)}) %collective-permute-start.19) | collective-permute-done | bytes 131104 | tf_op jit(solution)/shard_map/ppermute | solution.py:121
  81.8 12.8 %loss_rows.1 = (f32[104,1024]{1,0:T(8,128)S(1)}, f32[104,1024]{1,0:T(8,128)S(1)}, f32[1024,128]{1,0:T(8,128)S(1)}) custom-call(s32[3]{0:T(128)S(1)} %pad_add_fusion.ints, f32[1]{0:T(128)S(6)} %div.4.floats, s32[1024,1]{1,0:T(8,128)S(1)} %copy.64.token_col, s32[1024,1]{1,0:T(8,128)S(1)} %copy.65.target_col, s32[1,1024]{1,0:T(1,128)S(1)} %copy-done.1, ...), custom_call_target="tpu_custom_call" | custom-call | flops 13200000000 | bytes 12000000 | tf_op jit(solution)/shard_map/loss_rows/pallas_call | solution.py:799
  94.9 4.6 %attention_back.3 = f32[32,256]{1,0:T(8,128)S(1)} custom-call(s32[1024,1]{1,0:T(8,128)S(1)} %copy.64.token_col, s32[1,1024]{1,0:T(1,128)S(1)} %copy-done.1, bf16[2,1024,128]{2,1,0:T(8,128)(2,1)S(1)} %copy-done.49, bf16[2,1024,128]{2,1,0:T(8,128)(2,1)S(1)} %copy-done.51, f32[1024,128]{1,0:T(8,128)S(1)} %copy-done.57, ...), custom_call_target="tpu_custom_call" | custom-call | flops 6600000000 | bytes 6000000 | tf_op jit(solution)/shard_map/attention_back/pallas_call | solution.py:640
  99.6 1.2 collective-permute-start.26
  100.8 5.1 %attention_back.2 = f32[32,256]{1,0:T(8,128)S(1)} custom-call(s32[1024,1]{1,0:T(8,128)S(1)} %copy.64.token_col, s32[1,1024]{1,0:T(1,128)S(1)} %copy-done.1, bf16[2,1024,128]{2,1,0:T(8,128)(2,1)S(1)} %copy-done.53, bf16[2,1024,128]{2,1,0:T(8,128)(2,1)S(1)} %copy-done.55, f32[1024,128]{1,0:T(8,128)S(1)} %copy-done.57, ...), custom_call_target="tpu_custom_call" | custom-call | flops 6600000000 | bytes 6000000 | tf_op jit(solution)/shard_map/attention_back/pallas_call | solution.py:640
  108.5 5.5 %collective-permute-done.28 = f32[48,1024]{1,0:T(8,128)S(1)} collective-permute-done((f32[48,1024]{1,0:T(8,128)S(1)}, f32[48,1024]{1,0:T(8,128)S(1)}, u32[]{:S(2)}, u32[]{:S(2)}) %collective-permute-start.28) | collective-permute-done | bytes 196640 | tf_op jit(solution)/shard_map/ppermute | solution.py:121
  114.0 1.2 collective-permute-start.29
  115.2 4.6 %collective-permute-done.29 = f32[48,1024]{1,0:T(8,128)S(1)} collective-permute-done((f32[48,1024]{1,0:T(8,128)S(1)}, f32[48,1024]{1,0:T(8,128)S(1)}, u32[]{:S(2)}, u32[]{:S(2)}) %collective-permute-start.29) | collective-permute-done | bytes 196640 | tf_op jit(solution)/shard_map/ppermute | solution.py:121
  120.0 2.8 %copy-done.2 = bf16[192,128,128]{2,1,0:T(8,128)(2,1)S(1)} copy-done((bf16[192,128,128]{2,1,0:T(8,128)(2,1)S(1)}, bf16[192,128,128]{2,1,0:T(8,128)(2,1)}, u32[]{:S(2)}) %copy-start.2) | copy-done | bytes 6291480
  122.7 2.1 assemble.1
  124.8 1.1 copy-done.36
  126.0 1.3 copy-done.39
  127.3 1.3 copy-done.41
  128.6 1.1 collective-permute-start.32
  129.7 1.2 collective-permute-start.33
  130.8 1.3 collective-permute-start.34
  133.6 2.1 collective-permute-done.34
  135.8 1.4 copy-done.37
  137.2 1.6 copy-done.40
  138.8 1.6 copy-done.42
  140.4 13.6 %factors.1 = (bf16[18,192,128]{2,1,0:T(8,128)(2,1)S(1)}, bf16[34,192,128]{2,1,0:T(8,128)(2,1)S(1)}, f32[48,1024]{1,0:T(8,128)S(1)}, f32[1,1024]{1,0:T(1,128)S(1)}, f32[80,1024]{1,0:T(8,128)S(1)}) custom-call(s32[1]{0:T(128)} %bitcast.1.ints, f32[104,1024]{1,0:T(8,128)S(1)} %pad_maximum_fusion.mine, f32[104,1024]{1,0:T(8,128)S(1)} %collective-permute-done.31.other, ...), custom_call_target="tpu_custom_call" | custom-call | flops 7699999744 | bytes 7000000 | tf_op jit(solution)/shard_map/factors/pallas_call | solution.py:981
  154.8 2.3 %collective-permute-start.36 = (f32[24,1024]{1,0:T(8,128)S(1)}, f32[24,1024]{1,0:T(8,128)S(1)}, u32[]{:S(2)}, u32[]{:S(2)}) collective-permute-start(f32[24,1024]{1,0:T(8,128)S(1)} %get-tuple-element.187), channel_id=1, source_target_pairs={{0,1},{1,0},{2,3},{3,2},{4,5},{5,4},{6,7},{7,6},{8,9},{9,8},{10,11... | collective-permute-start | bytes 294920 | tf_op jit(solution)/shard_map/ppermute | solution.py:121
  158.1 1.4 collective-permute-start.38
  159.6 9.2 %gradient_products.1 = (f32[24,128,128]{2,1,0:T(8,128)S(1)}, f32[24,128,128]{2,1,0:T(8,128)S(1)}, f32[24,128,128]{2,1,0:T(8,128)S(1)}, f32[24,128,128]{2,1,0:T(8...) custom-call(s32[24]{0:T(128)S(1)} %copy-done.62, ...), custom_call_target="tpu_custom_call" | custom-call | flops 9900000256 | bytes 9000000 | tf_op jit(solution)/shard_map/gradient_products/pallas_call | solution.py:1260
  168.9 1.1 copy-done.43
  172.0 2.1 small.1
  174.7 37.2 %soap_tiles.1 = (f32[24,128,128]{2,1,0:T(8,128)}, bf16[24,128,128]{2,1,0:T(8,128)(2,1)}, f32[24,128,128]{2,1,0:T(8,128)}, f32[24,128,128]{2,1,0:T(8,128)}, f32[2...) custom-call(f32[2]{0:T(128)S(1)} %power_subtract_fusion.corrections, ...), custom_call_target="tpu_custom_call" | custom-call | flops 44000002048 | bytes 40000000 | tf_op jit(solution)/shard_map/soap_tiles/pallas_call | solution.py:1329
  (206 shorter events, 25.2 us)
Async XLA Ops:
  7.2 112.7 %all-gather.2.cloned.1.call-start = ((), (), s32[]{:S(2)}) async-start(), calls=%async_computation | async-start | bytes 7077888 | tf_op jit(solution)/shard_map/all_gather | solution.py:1388
  12.5 14.4 %copy-start = (bf16[24,128,128]{2,1,0:T(8,128)(2,1)S(1)}, bf16[24,128,128]{2,1,0:T(8,128)(2,1)}, u32[]{:S(2)}) copy-start(bf16[24,128,128]{2,1,0:T(8,128)(2,1)} %get-tuple-element.131.low) | copy-start | bytes 2359300
  12.5 14.4 %copy-start.22 = (f32[1,1024]{1,0:T(1,128)S(1)}, f32[1,1024]{1,0:T(1,128)}, u32[]{:S(2)}) copy-start(f32[1,1024]{1,0:T(1,128)} %refs_16_.1) | copy-start | bytes 12292
  12.6 1.7 collective-permute-start
  15.2 6.4 %collective-permute-start.1 = (f32[7,32,128]{2,1,0:T(8,128)S(1)}, f32[7,32,128]{2,1,0:T(8,128)S(1)}, u32[]{:S(2)}, u32[]{:S(2)}) collective-permute-start(f32[7,32,128]{2,1,0:T(8,128)S(1)} %add.53), channel_id=1, source_target_pairs={{0,8},{4,12},{8,0},{12,4},{16,24},{20,28},{24,16},{28,20},{1,9},{5... | collective-permute-start | bytes 344072 | tf_op jit(solution)/shard_map/ppermute | solution.py:121
  18.1 7.4 %collective-permute-start.2 = (f32[7,32,128]{2,1,0:T(8,128)S(1)}, f32[7,32,128]{2,1,0:T(8,128)S(1)}, u32[]{:S(2)}, u32[]{:S(2)}) collective-permute-start(f32[7,32,128]{2,1,0:T(8,128)S(1)} %add.53), channel_id=1, source_target_pairs={{0,16},{4,20},{8,24},{12,28},{16,0},{20,4},{24,8},{28,12},{1,17},{... | collective-permute-start | bytes 344072 | tf_op jit(solution)/shard_map/ppermute | solution.py:121
  19.6 5.9 %collective-permute-start.3 = (f32[7,32,128]{2,1,0:T(8,128)S(1)}, f32[7,32,128]{2,1,0:T(8,128)S(1)}, u32[]{:S(2)}, u32[]{:S(2)}) collective-permute-start(f32[7,32,128]{2,1,0:T(8,128)S(1)} %add.53), channel_id=1, source_target_pairs={{0,24},{4,28},{8,16},{12,20},{16,8},{20,12},{24,0},{28,4},{1,25},{... | collective-permute-start | bytes 344072 | tf_op jit(solution)/shard_map/ppermute | solution.py:121
  25.5 1.4 collective-permute-start.4
  28.7 4.2 %collective-permute-start.5 = (f32[640,128]{1,0:T(8,128)S(1)}, f32[640,128]{1,0:T(8,128)S(1)}, u32[]{:S(2)}, u32[]{:S(2)}) collective-permute-start(f32[640,128]{1,0:T(8,128)S(1)} %get-tuple-element.133), channel_id=1, source_target_pairs={{0,4},{4,0},{8,12},{12,8},{16,20},{20,16},{24,28},{28,24},{1,5},{5... | collective-permute-start | bytes 983048 | tf_op jit(solution)/shard_map/ppermute | solution.py:121
  33.1 6.6 %collective-permute-start.6 = (f32[160,128]{1,0:T(8,128)S(1)}, f32[160,128]{1,0:T(8,128)S(1)}, u32[]{:S(2)}, u32[]{:S(2)}) collective-permute-start(f32[160,128]{1,0:T(8,128)S(1)} %get-tuple-element.232), channel_id=1, source_target_pairs={{0,8},{4,12},{8,0},{12,4},{16,24},{20,28},{24,16},{28,20},{1,9},{5... | collective-permute-start | bytes 245768 | tf_op jit(solution)/shard_map/ppermute | solution.py:121
  34.4 12.9 %collective-permute-start.10 = (bf16[512,128]{1,0:T(8,128)(2,1)S(1)}, bf16[512,128]{1,0:T(8,128)(2,1)S(1)}, u32[]{:S(2)}, u32[]{:S(2)}) collective-permute-start(bf16[512,128]{1,0:T(8,128)(2,1)S(1)} %get-tuple-element.142.refs_0_), channel_id=1, source_target_pairs={{0,2},{1,3},{2,0},{3,1},{4,6},{5,7},{6,4},{7,5},{8,10},{9,11},{10,... | collective-permute-start | bytes 393224 | tf_op jit(solution)/shard_map/ppermute | solution.py:121
  37.0 10.3 %collective-permute-start.11 = (bf16[512,128]{1,0:T(8,128)(2,1)S(1)}, bf16[512,128]{1,0:T(8,128)(2,1)S(1)}, u32[]{:S(2)}, u32[]{:S(2)}) collective-permute-start(bf16[512,128]{1,0:T(8,128)(2,1)S(1)} %get-tuple-element.142.refs_0_), channel_id=1, source_target_pairs={{0,3},{1,2},{2,1},{3,0},{4,7},{5,6},{6,5},{7,4},{8,11},{9,10},{10,... | collective-permute-start | bytes 393224 | tf_op jit(solution)/shard_map/ppermute | solution.py:121
  38.3 9.4 %collective-permute-start.9 = (bf16[512,128]{1,0:T(8,128)(2,1)S(1)}, bf16[512,128]{1,0:T(8,128)(2,1)S(1)}, u32[]{:S(2)}, u32[]{:S(2)}) collective-permute-start(bf16[512,128]{1,0:T(8,128)(2,1)S(1)} %get-tuple-element.142.refs_0_), channel_id=1, source_target_pairs={{0,1},{1,0},{2,3},{3,2},{4,5},{5,4},{6,7},{7,6},{8,9},{9,8},{10,11... | collective-permute-start | bytes 393224 | tf_op jit(solution)/shard_map/ppermute | solution.py:121
  38.5 8.2 %collective-permute-start.7 = (f32[160,128]{1,0:T(8,128)S(1)}, f32[160,128]{1,0:T(8,128)S(1)}, u32[]{:S(2)}, u32[]{:S(2)}) collective-permute-start(f32[160,128]{1,0:T(8,128)S(1)} %get-tuple-element.231), channel_id=1, source_target_pairs={{0,16},{4,20},{8,24},{12,28},{16,0},{20,4},{24,8},{28,12},{1,17},{... | collective-permute-start | bytes 245768 | tf_op jit(solution)/shard_map/ppermute | solution.py:121
  39.6 7.5 %collective-permute-start.8 = (f32[160,128]{1,0:T(8,128)S(1)}, f32[160,128]{1,0:T(8,128)S(1)}, u32[]{:S(2)}, u32[]{:S(2)}) collective-permute-start(f32[160,128]{1,0:T(8,128)S(1)} %get-tuple-element.230), channel_id=1, source_target_pairs={{0,24},{4,28},{8,16},{12,20},{16,8},{20,12},{24,0},{28,4},{1,25},{... | collective-permute-start | bytes 245768 | tf_op jit(solution)/shard_map/ppermute | solution.py:121
  47.8 31.2 %copy-start.7 = (f32[1025,32]{0,1:T(8,128)S(1)}, f32[1025,32]{0,1:T(8,128)}, u32[]{:S(2)}) copy-start(f32[1025,32]{0,1:T(8,128)} %param.48) | copy-start | bytes 393604
  47.8 31.2 %copy-start.10 = (f32[32,1024]{1,0:T(8,128)S(1)}, f32[32,1024]{1,0:T(8,128)}, u32[]{:S(2)}) copy-start(f32[32,1024]{1,0:T(8,128)} %refs_7_.1) | copy-start | bytes 393220
  47.8 31.2 %copy-start.19 = (f32[5,1024]{1,0:T(8,128)S(1)}, f32[5,1024]{1,0:T(8,128)}, u32[]{:S(2)}) copy-start(f32[5,1024]{1,0:T(8,128)} %refs_13_.1) | copy-start | bytes 61444
  47.8 6.2 %collective-permute-start.12 = (f32[160,128]{1,0:T(8,128)S(1)}, f32[160,128]{1,0:T(8,128)S(1)}, u32[]{:S(2)}, u32[]{:S(2)}) collective-permute-start(f32[160,128]{1,0:T(8,128)S(1)} %add_add_fusion.1.refs_0_), channel_id=1, source_target_pairs={{0,1},{1,0},{2,3},{3,2},{4,5},{5,4},{6,7},{7,6},{8,9},{9,8},{10,11... | collective-permute-start | bytes 245768 | tf_op jit(solution)/shard_map/ppermute | solution.py:121
  50.0 6.3 %collective-permute-start.13 = (f32[160,128]{1,0:T(8,128)S(1)}, f32[160,128]{1,0:T(8,128)S(1)}, u32[]{:S(2)}, u32[]{:S(2)}) collective-permute-start(f32[160,128]{1,0:T(8,128)S(1)} %add_add_fusion.1.refs_0_), channel_id=1, source_target_pairs={{0,2},{1,3},{2,0},{3,1},{4,6},{5,7},{6,4},{7,5},{8,10},{9,11},{10,... | collective-permute-start | bytes 245768 | tf_op jit(solution)/shard_map/ppermute | solution.py:121
  52.0 8.2 %collective-permute-start.14 = (f32[160,128]{1,0:T(8,128)S(1)}, f32[160,128]{1,0:T(8,128)S(1)}, u32[]{:S(2)}, u32[]{:S(2)}) collective-permute-start(f32[160,128]{1,0:T(8,128)S(1)} %add_add_fusion.1.refs_0_), channel_id=1, source_target_pairs={{0,3},{1,2},{2,1},{3,0},{4,7},{5,6},{6,5},{7,4},{8,11},{9,10},{10,... | collective-permute-start | bytes 245768 | tf_op jit(solution)/shard_map/ppermute | solution.py:121
  53.4 12.8 %collective-permute-start.18 = (bf16[512,128]{1,0:T(8,128)(2,1)S(1)}, bf16[512,128]{1,0:T(8,128)(2,1)S(1)}, u32[]{:S(2)}, u32[]{:S(2)}) collective-permute-start(bf16[512,128]{1,0:T(8,128)(2,1)S(1)} %get-tuple-element.151.refs_4_), channel_id=1, source_target_pairs={{0,1},{1,0},{2,3},{3,2},{4,5},{5,4},{6,7},{7,6},{8,9},{9,8},{10,11... | collective-permute-start | bytes 393224 | tf_op jit(solution)/shard_map/ppermute | solution.py:121
  60.3 16.4 %collective-permute-start.15 = (bf16[608,128]{1,0:T(8,128)(2,1)S(1)}, bf16[608,128]{1,0:T(8,128)(2,1)S(1)}, u32[]{:S(2)}, u32[]{:S(2)}) collective-permute-start(bf16[608,128]{1,0:T(8,128)(2,1)S(1)} %pack_segments.1.refs_8_), channel_id=1, source_target_pairs={{0,8},{4,12},{8,0},{12,4},{16,24},{20,28},{24,16},{28,20},{1,9},{5... | collective-permute-start | bytes 466952 | tf_op jit(solution)/shard_map/ppermute | solution.py:121
  61.1 15.5 %collective-permute-start.16 = (bf16[608,128]{1,0:T(8,128)(2,1)S(1)}, bf16[608,128]{1,0:T(8,128)(2,1)S(1)}, u32[]{:S(2)}, u32[]{:S(2)}) collective-permute-start(bf16[608,128]{1,0:T(8,128)(2,1)S(1)} %pack_segments.1.refs_8_), channel_id=1, source_target_pairs={{0,16},{4,20},{8,24},{12,28},{16,0},{20,4},{24,8},{28,12},{1,17},{... | collective-permute-start | bytes 466952 | tf_op jit(solution)/shard_map/ppermute | solution.py:121
  62.6 14.1 %collective-permute-start.17 = (bf16[608,128]{1,0:T(8,128)(2,1)S(1)}, bf16[608,128]{1,0:T(8,128)(2,1)S(1)}, u32[]{:S(2)}, u32[]{:S(2)}) collective-permute-start(bf16[608,128]{1,0:T(8,128)(2,1)S(1)} %pack_segments.1.refs_8_), channel_id=1, source_target_pairs={{0,24},{4,28},{8,16},{12,20},{16,8},{20,12},{24,0},{28,4},{1,25},{... | collective-permute-start | bytes 466952 | tf_op jit(solution)/shard_map/ppermute | solution.py:121
  63.8 11.6 %collective-permute-start.19 = (bf16[512,128]{1,0:T(8,128)(2,1)S(1)}, bf16[512,128]{1,0:T(8,128)(2,1)S(1)}, u32[]{:S(2)}, u32[]{:S(2)}) collective-permute-start(bf16[512,128]{1,0:T(8,128)(2,1)S(1)} %get-tuple-element.151.refs_4_), channel_id=1, source_target_pairs={{0,2},{1,3},{2,0},{3,1},{4,6},{5,7},{6,4},{7,5},{8,10},{9,11},{10,... | collective-permute-start | bytes 393224 | tf_op jit(solution)/shard_map/ppermute | solution.py:121
  66.9 9.1 %collective-permute-start.20 = (bf16[512,128]{1,0:T(8,128)(2,1)S(1)}, bf16[512,128]{1,0:T(8,128)(2,1)S(1)}, u32[]{:S(2)}, u32[]{:S(2)}) collective-permute-start(bf16[512,128]{1,0:T(8,128)(2,1)S(1)} %get-tuple-element.151.refs_4_), channel_id=1, source_target_pairs={{0,3},{1,2},{2,1},{3,0},{4,7},{5,6},{6,5},{7,4},{8,11},{9,10},{10,... | collective-permute-start | bytes 393224 | tf_op jit(solution)/shard_map/ppermute | solution.py:121
  76.7 2.2 collective-permute-start.21
  76.8 2.1 collective-permute-start.22
  77.3 1.6 collective-permute-start.23
  77.3 1.7 collective-permute-start.24
  94.6 4.9 %collective-permute-start.25 = (f32[104,1024]{1,0:T(8,128)S(1)}, f32[104,1024]{1,0:T(8,128)S(1)}, u32[]{:S(2)}, u32[]{:S(2)}) collective-permute-start(f32[104,1024]{1,0:T(8,128)S(1)} %get-tuple-element.161), channel_id=1, source_target_pairs={{0,4},{4,0},{8,12},{12,8},{16,20},{20,16},{24,28},{28,24},{1,5},{5... | collective-permute-start | bytes 1277960 | tf_op jit(solution)/shard_map/ppermute | solution.py:121
  99.6 7.9 %collective-permute-start.26 = (f32[56,1024]{1,0:T(8,128)S(1)}, f32[56,1024]{1,0:T(8,128)S(1)}, u32[]{:S(2)}, u32[]{:S(2)}) collective-permute-start(f32[56,1024]{1,0:T(8,128)S(1)} %slice.38), channel_id=1, source_target_pairs={{0,8},{4,12},{8,0},{12,4},{16,24},{20,28},{24,16},{28,20},{1,9},{5... | collective-permute-start | bytes 688136 | tf_op jit(solution)/shard_map/ppermute | solution.py:121
  106.0 9.2 %collective-permute-start.30 = (f32[32,256]{1,0:T(8,128)S(1)}, f32[32,256]{1,0:T(8,128)S(1)}, u32[]{:S(2)}, u32[]{:S(2)}) collective-permute-start(f32[32,256]{1,0:T(8,128)S(1)} %broadcast_select_fusion), channel_id=1, source_target_pairs={{0,4},{4,0},{8,12},{12,8},{16,20},{20,16},{24,28},{28,24},{1,5},{5... | collective-permute-start | bytes 98312 | tf_op jit(solution)/shard_map/ppermute | solution.py:121
  106.3 7.7 %collective-permute-start.28 = (f32[48,1024]{1,0:T(8,128)S(1)}, f32[48,1024]{1,0:T(8,128)S(1)}, u32[]{:S(2)}, u32[]{:S(2)}) collective-permute-start(f32[48,1024]{1,0:T(8,128)S(1)} %slice.39), channel_id=1, source_target_pairs={{0,16},{4,20},{8,24},{12,28},{16,0},{20,4},{24,8},{28,12},{1,17},{... | collective-permute-start | bytes 589832 | tf_op jit(solution)/shard_map/ppermute | solution.py:121
  107.6 12.3 %collective-permute-start.27 = (f32[56,1024]{1,0:T(8,128)S(1)}, f32[56,1024]{1,0:T(8,128)S(1)}, u32[]{:S(2)}, u32[]{:S(2)}) collective-permute-start(f32[56,1024]{1,0:T(8,128)S(1)} %slice_add_fusion.1), channel_id=1, source_target_pairs={{0,16},{4,20},{8,24},{12,28},{16,0},{20,4},{24,8},{28,12},{1,17},{... | collective-permute-start | bytes 688136 | tf_op jit(solution)/shard_map/ppermute | solution.py:121
  114.0 5.8 %collective-permute-start.29 = (f32[48,1024]{1,0:T(8,128)S(1)}, f32[48,1024]{1,0:T(8,128)S(1)}, u32[]{:S(2)}, u32[]{:S(2)}) collective-permute-start(f32[48,1024]{1,0:T(8,128)S(1)} %slice_add_fusion), channel_id=1, source_target_pairs={{0,8},{4,12},{8,0},{12,4},{16,24},{20,28},{24,16},{28,20},{1,9},{5... | collective-permute-start | bytes 589832 | tf_op jit(solution)/shard_map/ppermute | solution.py:121
  128.6 7.1 %collective-permute-start.31 = (f32[104,1024]{1,0:T(8,128)S(1)}, f32[104,1024]{1,0:T(8,128)S(1)}, u32[]{:S(2)}, u32[]{:S(2)}) collective-permute-start(f32[104,1024]{1,0:T(8,128)S(1)} %pad_maximum_fusion.mine), channel_id=1, source_target_pairs={{0,4},{4,0},{8,12},{12,8},{16,20},{20,16},{24,28},{28,24},{1,5},{5... | collective-permute-start | bytes 1277960 | tf_op jit(solution)/shard_map/ppermute | solution.py:121
  128.6 4.1 %collective-permute-start.32 = (f32[32,256]{1,0:T(8,128)S(1)}, f32[32,256]{1,0:T(8,128)S(1)}, u32[]{:S(2)}, u32[]{:S(2)}) collective-permute-start(f32[32,256]{1,0:T(8,128)S(1)} %select_add_fusion), channel_id=1, source_target_pairs={{0,8},{4,12},{8,0},{12,4},{16,24},{20,28},{24,16},{28,20},{1,9},{5... | collective-permute-start | bytes 98312 | tf_op jit(solution)/shard_map/ppermute | solution.py:121
  129.7 3.9 %collective-permute-start.33 = (f32[32,256]{1,0:T(8,128)S(1)}, f32[32,256]{1,0:T(8,128)S(1)}, u32[]{:S(2)}, u32[]{:S(2)}) collective-permute-start(f32[32,256]{1,0:T(8,128)S(1)} %select_add_fusion), channel_id=1, source_target_pairs={{0,16},{4,20},{8,24},{12,28},{16,0},{20,4},{24,8},{28,12},{1,17},{... | collective-permute-start | bytes 98312 | tf_op jit(solution)/shard_map/ppermute | solution.py:121
  130.8 4.8 %collective-permute-start.34 = (f32[32,256]{1,0:T(8,128)S(1)}, f32[32,256]{1,0:T(8,128)S(1)}, u32[]{:S(2)}, u32[]{:S(2)}) collective-permute-start(f32[32,256]{1,0:T(8,128)S(1)} %select_add_fusion), channel_id=1, source_target_pairs={{0,24},{4,28},{8,16},{12,20},{16,8},{20,12},{24,0},{28,4},{1,25},{... | collective-permute-start | bytes 98312 | tf_op jit(solution)/shard_map/ppermute | solution.py:121
  135.7 18.3 %collective-permute-start.35 = (f32[32,256]{1,0:T(8,128)S(1)}, f32[32,256]{1,0:T(8,128)S(1)}, u32[]{:S(2)}, u32[]{:S(2)}) collective-permute-start(f32[32,256]{1,0:T(8,128)S(1)} %add_add_fusion.2.mine), channel_id=1, source_target_pairs={{0,4},{4,0},{8,12},{12,8},{16,20},{20,16},{24,28},{28,24},{1,5},{5... | collective-permute-start | bytes 98312 | tf_op jit(solution)/shard_map/ppermute | solution.py:121
  154.8 15.3 %collective-permute-start.36 = (f32[24,1024]{1,0:T(8,128)S(1)}, f32[24,1024]{1,0:T(8,128)S(1)}, u32[]{:S(2)}, u32[]{:S(2)}) collective-permute-start(f32[24,1024]{1,0:T(8,128)S(1)} %get-tuple-element.187), channel_id=1, source_target_pairs={{0,1},{1,0},{2,3},{3,2},{4,5},{5,4},{6,7},{7,6},{8,9},{9,8},{10,11... | collective-permute-start | bytes 294920 | tf_op jit(solution)/shard_map/ppermute | solution.py:121
  157.1 13.0 %collective-permute-start.37 = (f32[24,1024]{1,0:T(8,128)S(1)}, f32[24,1024]{1,0:T(8,128)S(1)}, u32[]{:S(2)}, u32[]{:S(2)}) collective-permute-start(f32[24,1024]{1,0:T(8,128)S(1)} %get-tuple-element.187), channel_id=1, source_target_pairs={{0,2},{1,3},{2,0},{3,1},{4,6},{5,7},{6,4},{7,5},{8,10},{9,11},{10,... | collective-permute-start | bytes 294920 | tf_op jit(solution)/shard_map/ppermute | solution.py:121
  158.1 12.0 %collective-permute-start.38 = (f32[24,1024]{1,0:T(8,128)S(1)}, f32[24,1024]{1,0:T(8,128)S(1)}, u32[]{:S(2)}, u32[]{:S(2)}) collective-permute-start(f32[24,1024]{1,0:T(8,128)S(1)} %get-tuple-element.187), channel_id=1, source_target_pairs={{0,3},{1,2},{2,1},{3,0},{4,7},{5,6},{6,5},{7,4},{8,11},{9,10},{10,... | collective-permute-start | bytes 294920 | tf_op jit(solution)/shard_map/ppermute | solution.py:121
  170.0 1.4 collective-permute-start.39
  170.1 1.4 collective-permute-start.40
  170.6 1.3 collective-permute-start.41
  (59 other events, 439.3 us)
Sparse Core Ops, SparseCore 0:
  25.6 56.0 all-gather.1
where the time goes:
time: 222 us; the launch traced here: 219 us
  Pallas kernels  102 us (46%)
  starting transfers between devices  40.9 us (18%)
  waiting for transfers between devices  37.3 us (17%)
  local copies, waits for them, and re-layouts  20.3 us (9%)
  between operations  16.5 us (7%)
    ppermute x42, starting transfers between devices, swap_with(): return lax.ppermute(value, axis, [(i, i ^ mask) for i in range(count)])  40.9 us
    ppermute x42, waiting for transfers between devices, swap_with(): return lax.ppermute(value, axis, [(i, i ^ mask) for i in range(count)])  37.2 us
    pallas_call x1, Pallas kernels, soap(): pl.pallas_call(functools.partial(soap_kernel, count, PER), grid=(count //...  37.2 us
    unnamed x128, local copies, waits for them, and re-layouts  18.6 us
    pallas_call x1, Pallas kernels, factors(): pl.pallas_call(functools.partial(factors_kernel, heads), in_specs=[SMEM]...  13.6 us
    pallas_call x1, Pallas kernels, loss_rows(): pl.pallas_call(functools.partial(loss_kernel, parts, len(pieces), heads),...  12.8 us
    pallas_call x2, Pallas kernels, attention_back(): pl.pallas_call(functools.partial(attention_back_kernel, heads, pair), gri...  9.73 us
    pallas_call x1, Pallas kernels, gradient_products(): pl.pallas_call(functools.partial(gradient_kernel, PER, more.shape[0]), gr...  9.22 us
  transfers between devices with their start and end apart: 43, of which 21 were waited for; matrix products, arithmetic and copies ran while one was open for 1% of the time, Pallas kernels for 25%

commit v1 on v0

--- a/solution.py
+++ b/solution.py
@@ -378,23 +378,6 @@
         name="pack_segments",
         **params(1),
     )(*parts)
-
-
-def assemble_kernel(places, owner, tiles, *mats):
-    for index, (which, i, k) in enumerate(places):
-        mats[which][i * BS : (i + 1) * BS, k * BS : (k + 1) * BS] = tiles[owner[index]]
-
-
-def assemble(owner, tiles, heads, ff_local):
-    shapes = layer_shapes(heads, ff_local)
-    return pl.pallas_call(
-        functools.partial(assemble_kernel, tile_places(shapes)),
-        in_specs=[SMEM, VMEM],
-        out_specs=[VMEM] * 4,
-        out_shape=[jax.ShapeDtypeStruct(shape, bf16) for shape in shapes],
-        name="assemble",
-        **params(5),
-    )(owner, tiles)
 
 
 def rotary_tables(seq_len):
@@ -850,12 +833,10 @@
 def factors_kernel(
     heads,
     ints,
+    owner,
     mine,
     other,
-    mat_q,
-    mat_o,
-    mat_u,
-    mat_f,
+    tiles,
     upper,
     normed,
     act,
@@ -865,10 +846,16 @@
     hidden_o,
     bias_o,
     small_o,
+    part_o,
     sums,
+    *mats,
 ):
     vocab = normed.shape[0]
-    width = mat_u.shape[1]
+    width = upper.shape[1]
+    for index, (which, i, k) in enumerate(tile_places(layer_shapes(heads, width))):
+        mats[which][i * BS : (i + 1) * BS, k * BS : (k + 1) * BS] = tiles[owner[index]]
+    mat_q, mat_o, mat_u, mat_f = mats
+    part_o[...] = mat_q[:, : 2 * heads * HD]
     join(ints[0] & 1, mine, other, sums)
     small_o[...] = sums[: small_o.shape[0]]
     rows = sums[0:vocab]
@@ -944,7 +931,7 @@
         put_right(right_o, k, block)
     low = normed[...].astype(f32)
     square = jnp.sum(dot6(low, low, NT) * dot6(grad, grad, NT), keepdims=True)
-    hidden_o[0:vocab] = hidden[0:vocab] + rows_times_low(grad, mat_q[:, : 2 * pairs * WIDE], NT)
+    hidden_o[0:vocab] = hidden[0:vocab] + rows_times_low(grad, mat_q[...], NT)
     hidden_o[vocab:] = hidden[vocab:] + square
     size = half_o.shape[0]
     half_o[...] = hidden_o[pl.ds(pl.multiple_of((ints[0] & 1) * size, size), size)]
@@ -972,7 +959,7 @@
     return np.array(left, np.int32), np.array(right, np.int32)
 
 
-def factors(ints, mine, other, mats, upper, normed, act, values, heads):
+def factors(ints, owner, mine, other, tiles, upper, normed, act, values, heads):
     vocab = normed.shape[0]
     ff_local = upper.shape[1]
     n_left = D // BS + ff_local // BS + heads // 2
@@ -980,19 +967,21 @@
     o = jax.ShapeDtypeStruct
     return pl.pallas_call(
         functools.partial(factors_kernel, heads),
-        in_specs=[SMEM] + [VMEM] * 10,
-        out_specs=[VMEM] * 5,
+        in_specs=[SMEM] * 2 + [VMEM] * 7,
+        out_specs=[VMEM] * 6,
         out_shape=[
             o((n_left, 3 * HB, BS), bf16),
             o((n_right, 3 * HB, BS), bf16),
             o((vocab + 16, D), f32),
             o((1, ff_local), f32),
             o((2 * vocab + 16, D), f32),
+            o((D, 2 * heads * HD), bf16),
         ],
-        scratch_shapes=[pltpu.VMEM((2 * mine.shape[0], D), f32)],
+        scratch_shapes=[pltpu.VMEM((2 * mine.shape[0], D), f32)]
+        + [pltpu.VMEM(shape, bf16) for shape in layer_shapes(heads, ff_local)],
         name="factors",
         **params(7),
-    )(ints, mine, other, *mats, upper, normed, act, values)
+    )(ints, owner, mine, other, tiles, upper, normed, act, values)
 
 
 def factors_rest(ints, mine, other, hidden, mat_q, normed, heads):
@@ -1336,7 +1325,7 @@
         + [pltpu.VMEM((2 * count, BS, BS), f32)] * 2
         + [pltpu.VMEM((count // 2, QB, BS), f32)],
         name="soap_tiles",
-        **params(40, 48),
+        **params(40, 36),
     )(corrections, scal, *products, W, m, v, L, R, QL, QR)
 
 
@@ -1416,7 +1405,6 @@
     packed = pack_segments(heads, dp_count, gather_xor(mine, "mp"))
     even = [packed] + [swap_with(packed, "dp", 2 * q) for q in places]
     if heads > 2:
-        even, more = lax.optimization_barrier((even, more))
         weights = weights + more
     odd = [swap_with(piece, "dp", 1) for piece in even]
     pieces = [piece for two in zip(even, odd) for piece in two]
@@ -1464,15 +1452,12 @@
     table = jnp.where(is_upper, second, first) + swap_with(
         jnp.where(is_upper, first, second), "dp", 1
     )
-    gathered, table = lax.optimization_barrier((gathered, table))
-    mats = assemble(tile_owner, gathered, heads, ff_local)
     table = direct(table)
-    mine, mats = lax.optimization_barrier((mine, mats))
-    left, right, hidden, bias_grad, sums = factors(
-        own_index, mine, swap_with(mine, "dp", 1), mats, upper, normed, act, values, heads
+    left, right, hidden, bias_grad, sums, mat_part = factors(
+        own_index, tile_owner, mine, swap_with(mine, "dp", 1), gathered, upper, normed, act, values, heads
     )
     more, hidden, hidden_half = factors_rest(
-        own_index, table, swap_with(table, "dp", 1), hidden, mats[0], normed, heads
+        own_index, table, swap_with(table, "dp", 1), hidden, mat_part, normed, heads
     )
     hidden_parts = gather_halves(hidden_half)
     left_at, right_at = (jnp.asarray(places) for places in factor_places(heads, ff_local))

time: 222 us -> 206 us (0.928)
  local copies, waits for them, and re-layouts: 20.3 us -> 10.9 us
  waiting for transfers between devices: 37.3 us -> 30.1 us
    unnamed x128 -> x112, local copies, waits for them, and re-layouts: 18.6 us -> 9.19 us
    ppermute x42, waiting for transfers between devices: 37.2 us -> 30.1 us  [swap_with(): return lax.ppermute(value, axis, [(i, i ^ mask) for i in range(count)])]
    pallas_call x1, Pallas kernels: 37.2 us -> 34.9 us  [soap(): pl.pallas_call(functools.partial(soap_kernel, count, PER), grid=(count //...]
  transfers between devices with their start and end apart: 43 -> 43, of which waited for: 21 -> 21; matrix products, arithmetic and copies ran while one was open for 1% -> 1% of each run, Pallas kernels for 25% -> 28%
where the time goes in v1:
time: 206 us; the launch traced here: 203 us
  Pallas kernels  100 us (49%)
  starting transfers between devices  42.9 us (21%)
  waiting for transfers between devices  30.1 us (15%)
  between operations  16.5 us (8%)
  local copies, waits for them, and re-layouts  10.9 us (5%)
  other arithmetic  2.06 us (1%)
    ppermute x42, starting transfers between devices, swap_with(): return lax.ppermute(value, axis, [(i, i ^ mask) for i in range(count)])  42.9 us
    pallas_call x1, Pallas kernels, soap(): pl.pallas_call(functools.partial(soap_kernel, count, PER), grid=(count //...  34.9 us
    ppermute x42, waiting for transfers between devices, swap_with(): return lax.ppermute(value, axis, [(i, i ^ mask) for i in range(count)])  30.1 us
    pallas_call x1, Pallas kernels, factors(): pl.pallas_call(functools.partial(factors_kernel, heads), in_specs=[SMEM]...  15.7 us
    pallas_call x1, Pallas kernels, loss_rows(): pl.pallas_call(functools.partial(loss_kernel, parts, len(pieces), heads),...  13.4 us
    pallas_call x2, Pallas kernels, attention_back(): pl.pallas_call(functools.partial(attention_back_kernel, heads, pair), gri...  9.75 us
    pallas_call x1, Pallas kernels, gradient_products(): pl.pallas_call(functools.partial(gradient_kernel, PER, more.shape[0]), gr...  9.22 us
    unnamed x112, local copies, waits for them, and re-layouts  9.19 us
  transfers between devices with their start and end apart: 43, of which 21 were waited for; matrix products, arithmetic and copies ran while one was open for 1% of the time, Pallas kernels for 28%

profile of v1, /device:TPU:0, one launch (start us, length us, event | category | flops | bytes accessed | tf_op | source)
XLA Modules:
  0.0 202.6 jit_solution(6902812935593567527)
XLA Ops:
  7.2 5.2 %first_tables.1 = (s32[24]{0:T(128)}, bf16[24,128,128]{2,1,0:T(8,128)(2,1)}, bf16[32,1024]{1,0:T(8,128)(2,1)}, f32[7,32,128]{2,1,0:T(8,128)}, f32[7,32,128]{2,1,0:T(8,128)}) custom-call(s32[192]{0:T(256)} %owner.3, s32[1]{0:T(128)} %bitcast.1.ints, s32[192]{0:T(256)} %constant.45.clone.row_of, s32[192]{0:T(256)} %constant.46.clone.block_of, ...), custom_call_target="tpu_custom_call" | custom-call | flops 4400000000 | bytes 4000000 | tf_op jit(solution)/shard_map/first_tables/pallas_call | solution.py:249
  13.1 1.2 collective-permute-done
  14.2 0.9 add.53
  15.2 2.9 %collective-permute-start.1 = (f32[7,32,128]{2,1,0:T(8,128)S(1)}, f32[7,32,128]{2,1,0:T(8,128)S(1)}, u32[]{:S(2)}, u32[]{:S(2)}) collective-permute-start(f32[7,32,128]{2,1,0:T(8,128)S(1)} %add.53), channel_id=1, source_target_pairs={{0,8},{4,12},{8,0},{12,4},{16,24},{20,28},{24,16},{28,20},{1,9},{5... | collective-permute-start | bytes 344072 | tf_op jit(solution)/shard_map/ppermute | solution.py:121
  18.1 1.5 collective-permute-start.2
  19.6 2.0 collective-permute-done.1
  21.6 3.9 %collective-permute-done.2 = f32[7,32,128]{2,1,0:T(8,128)S(1)} collective-permute-done((f32[7,32,128]{2,1,0:T(8,128)S(1)}, f32[7,32,128]{2,1,0:T(8,128)S(1)}, u32[]{:S(2)}, u32[]{:S(2)}) %collective-permute-start.2) | collective-permute-done | bytes 114720 | tf_op jit(solution)/shard_map/ppermute | solution.py:121
  27.0 1.1 second_tables.1
  28.9 4.0 %attention.2 = (bf16[2,1024,128]{2,1,0:T(8,128)(2,1)S(1)}, bf16[2,1024,128]{2,1,0:T(8,128)(2,1)S(1)}, f32[1024,128]{1,0:T(8,128)S(1)}, bf16[512,128]{1,0:T(8,128)(2,1)S(1)}) custom-call(s32[1]{0:T(128)S(6)} %copy.68.length, s32[1024,1]{1,0:T(8,128)S(1)} %copy.64.token_col, f32[32,768]{1,0:T(8,128)S(1)} %get-tuple-element.116.proj, ...), custom_call_target="tpu_custom_call" | custom-call | flops 6600000000 | bytes 6000000 | tf_op jit(solution)/shard_map/attention/pallas_call | solution.py:508
  33.1 1.3 collective-permute-start.6
  34.4 2.6 %collective-permute-start.10 = (bf16[512,128]{1,0:T(8,128)(2,1)S(1)}, bf16[512,128]{1,0:T(8,128)(2,1)S(1)}, u32[]{:S(2)}, u32[]{:S(2)}) collective-permute-start(bf16[512,128]{1,0:T(8,128)(2,1)S(1)} %get-tuple-element.124.refs_0_), channel_id=1, source_target_pairs={{0,2},{1,3},{2,0},{3,1},{4,6},{5,7},{6,4},{7,5},{8,10},{9,11},{10,... | collective-permute-start | bytes 393224 | tf_op jit(solution)/shard_map/ppermute | solution.py:121
  37.0 1.3 collective-permute-start.11
  39.6 1.5 collective-permute-start.8
  41.1 4.0 %attention.3 = (bf16[2,1024,128]{2,1,0:T(8,128)(2,1)S(1)}, bf16[2,1024,128]{2,1,0:T(8,128)(2,1)S(1)}, f32[1024,128]{1,0:T(8,128)S(1)}, bf16[512,128]{1,0:T(8,128)(2,1)S(1)}) custom-call(s32[1]{0:T(128)S(6)} %copy.68.length, s32[1024,1]{1,0:T(8,128)S(1)} %copy.64.token_col, f32[32,768]{1,0:T(8,128)S(1)} %get-tuple-element.116.proj, ...), custom_call_target="tpu_custom_call" | custom-call | flops 6600000000 | bytes 6000000 | tf_op jit(solution)/shard_map/attention/pallas_call | solution.py:508
  47.8 2.2 %collective-permute-start.15 = (f32[160,128]{1,0:T(8,128)S(1)}, f32[160,128]{1,0:T(8,128)S(1)}, u32[]{:S(2)}, u32[]{:S(2)}) collective-permute-start(f32[160,128]{1,0:T(8,128)S(1)} %add_add_fusion.1.refs_0_), channel_id=1, source_target_pairs={{0,1},{1,0},{2,3},{3,2},{4,5},{5,4},{6,7},{7,6},{8,9},{9,8},{10,11... | collective-permute-start | bytes 245768 | tf_op jit(solution)/shard_map/ppermute | solution.py:121
  50.0 2.0 collective-permute-start.16
  52.0 1.4 collective-permute-start.17
  53.4 2.9 %collective-permute-done.16.refs_2_ = f32[160,128]{1,0:T(8,128)S(1)} collective-permute-done((f32[160,128]{1,0:T(8,128)S(1)}, f32[160,128]{1,0:T(8,128)S(1)}, u32[]{:S(2)}, u32[]{:S(2)}) %collective-permute-start.16) | collective-permute-done | bytes 81952 | tf_op jit(solution)/shard_map/ppermute | solution.py:121
  56.4 3.0 %collective-permute-done.17.refs_3_ = f32[160,128]{1,0:T(8,128)S(1)} collective-permute-done((f32[160,128]{1,0:T(8,128)S(1)}, f32[160,128]{1,0:T(8,128)S(1)}, u32[]{:S(2)}, u32[]{:S(2)}) %collective-permute-start.17) | collective-permute-done | bytes 81952 | tf_op jit(solution)/shard_map/ppermute | solution.py:121
  59.4 1.0 collective-permute-start.19
  60.4 1.4 collective-permute-start.21
  61.8 1.2 collective-permute-start.23
  62.9 1.9 collective-permute-start.12
  64.8 1.4 collective-permute-start.13
  66.8 2.6 %collective-permute-done.12.refs_5_ = bf16[512,128]{1,0:T(8,128)(2,1)S(1)} collective-permute-done((bf16[512,128]{1,0:T(8,128)(2,1)S(1)}, bf16[512,128]{1,0:T(8,128)(2,1)S(1)}, u32[]{:S(2)}, u32[]{:S(2)}) %collective-permute-start.12) | collective-permute-done | bytes 131104 | tf_op jit(solution)/shard_map/ppermute | solution.py:121
  70.0 2.2 %collective-permute-start.14 = (bf16[512,128]{1,0:T(8,128)(2,1)S(1)}, bf16[512,128]{1,0:T(8,128)(2,1)}, u32[]{:S(2)}, u32[]{:S(2)}) collective-permute-start(bf16[512,128]{1,0:T(8,128)(2,1)S(1)} %get-tuple-element.128.refs_4_), channel_id=1, source_target_pairs={{0,3},{1,2},{2,1},{3,0},{4,7},{5,6},{6,5},{7,4},{8,11},{9,10},{10,... | collective-permute-start | bytes 393224 | tf_op jit(solution)/shard_map/ppermute | solution.py:121
  72.2 2.7 %collective-permute-done.13.refs_6_ = bf16[512,128]{1,0:T(8,128)(2,1)S(1)} collective-permute-done((bf16[512,128]{1,0:T(8,128)(2,1)S(1)}, bf16[512,128]{1,0:T(8,128)(2,1)S(1)}, u32[]{:S(2)}, u32[]{:S(2)}) %collective-permute-start.13) | collective-permute-done | bytes 131104 | tf_op jit(solution)/shard_map/ppermute | solution.py:121
  78.0 0.9 copy-done.17
  78.9 0.9 copy-done.19
  79.8 13.4 %loss_rows.1 = (f32[104,1024]{1,0:T(8,128)S(1)}, f32[104,1024]{1,0:T(8,128)S(1)}, f32[1024,128]{1,0:T(8,128)S(1)}) custom-call(s32[3]{0:T(128)S(1)} %pad_add_fusion.ints, f32[1]{0:T(128)S(6)} %div.4.floats, s32[1024,1]{1,0:T(8,128)S(1)} %copy.64.token_col, s32[1024,1]{1,0:T(8,128)S(1)} %copy.65.target_col, s32[1,1024]{1,0:T(1,128)S(1)} %copy-done.1, ...), custom_call_target="tpu_custom_call" | custom-call | flops 13200000000 | bytes 12000000 | tf_op jit(solution)/shard_map/loss_rows/pallas_call | solution.py:782
  93.7 4.6 %attention_back.3 = f32[32,256]{1,0:T(8,128)S(1)} custom-call(s32[1024,1]{1,0:T(8,128)S(1)} %copy.64.token_col, s32[1,1024]{1,0:T(1,128)S(1)} %copy-done.1, bf16[2,1024,128]{2,1,0:T(8,128)(2,1)S(1)} %copy-done.41, bf16[2,1024,128]{2,1,0:T(8,128)(2,1)S(1)} %copy-done.43, f32[1024,128]{1,0:T(8,128)S(1)} %copy-done.49, ...), custom_call_target="tpu_custom_call" | custom-call | flops 6600000000 | bytes 6000000 | tf_op jit(solution)/shard_map/attention_back/pallas_call | solution.py:623
  99.2 1.4 collective-permute-start.28
  100.6 5.1 %attention_back.2 = f32[32,256]{1,0:T(8,128)S(1)} custom-call(s32[1024,1]{1,0:T(8,128)S(1)} %copy.64.token_col, s32[1,1024]{1,0:T(1,128)S(1)} %copy-done.1, bf16[2,1024,128]{2,1,0:T(8,128)(2,1)S(1)} %copy-done.45, bf16[2,1024,128]{2,1,0:T(8,128)(2,1)S(1)} %copy-done.47, f32[1024,128]{1,0:T(8,128)S(1)} %copy-done.49, ...), custom_call_target="tpu_custom_call" | custom-call | flops 6600000000 | bytes 6000000 | tf_op jit(solution)/shard_map/attention_back/pallas_call | solution.py:623
  107.0 1.5 collective-permute-start.29
  108.5 4.6 %collective-permute-done.29 = f32[48,1024]{1,0:T(8,128)S(1)} collective-permute-done((f32[48,1024]{1,0:T(8,128)S(1)}, f32[48,1024]{1,0:T(8,128)S(1)}, u32[]{:S(2)}, u32[]{:S(2)}) %collective-permute-start.29) | collective-permute-done | bytes 196640 | tf_op jit(solution)/shard_map/ppermute | solution.py:121
  113.4 1.4 collective-permute-start.32
  114.8 0.9 collective-permute-start.33
  115.7 1.2 collective-permute-start.34
  117.6 1.1 collective-permute-done.33
  118.7 1.8 collective-permute-done.34
  120.7 2.8 %copy-done.2 = bf16[192,128,128]{2,1,0:T(8,128)(2,1)S(1)} copy-done((bf16[192,128,128]{2,1,0:T(8,128)(2,1)S(1)}, bf16[192,128,128]{2,1,0:T(8,128)(2,1)}, u32[]{:S(2)}) %copy-start.2) | copy-done | bytes 6291480
  123.5 15.7 %factors.1 = (bf16[18,192,128]{2,1,0:T(8,128)(2,1)S(1)}, bf16[34,192,128]{2,1,0:T(8,128)(2,1)S(1)}, f32[48,1024]{1,0:T(8,128)S(1)}, f32[1,1024]{1,0:T(1,128)S(1)...) custom-call(s32[1]{0:T(128)} %bitcast.1.ints, s32[192]{0:T(256)S(1)} %copy-done.26, ...), custom_call_target="tpu_custom_call" | custom-call | flops 7699999744 | bytes 7000000 | tf_op jit(solution)/shard_map/factors/pallas_call | solution.py:968
  139.9 2.0 collective-permute-start.36
  141.9 3.1 %collective-permute-start.37 = (f32[24,1024]{1,0:T(8,128)S(1)}, f32[24,1024]{1,0:T(8,128)S(1)}, u32[]{:S(2)}, u32[]{:S(2)}) collective-permute-start(f32[24,1024]{1,0:T(8,128)S(1)} %get-tuple-element.151), channel_id=1, source_target_pairs={{0,2},{1,3},{2,0},{3,1},{4,6},{5,7},{6,4},{7,5},{8,10},{9,11},{10,... | collective-permute-start | bytes 294920 | tf_op jit(solution)/shard_map/ppermute | solution.py:121
  145.2 9.2 %gradient_products.1 = (f32[24,128,128]{2,1,0:T(8,128)S(1)}, f32[24,128,128]{2,1,0:T(8,128)S(1)}, f32[24,128,128]{2,1,0:T(8,128)S(1)}, f32[24,128,128]{2,1,0:T(8...) custom-call(s32[24]{0:T(128)S(1)} %copy-done.54, ...), custom_call_target="tpu_custom_call" | custom-call | flops 9900000256 | bytes 9000000 | tf_op jit(solution)/shard_map/gradient_products/pallas_call | solution.py:1249
  154.4 1.1 copy-done.37
  157.5 2.1 %small.1 = (f32[32,1024]{1,0:T(8,128)}, f32[32,1024]{1,0:T(8,128)}, f32[32,1024]{1,0:T(8,128)}, f32[32,1025]{1,0:T(8,128)}, f32[32,1025]{1,0:T(8,128)}, /*index=...) custom-call(f32[2]{0:T(128)S(1)} %power_subtract_fusion.corrections,, ...), custom_call_target="tpu_custom_call" | custom-call | flops 4400000000 | bytes 4000000 | tf_op jit(solution)/shard_map/small/pallas_call | solution.py:1070
  160.7 34.9 %soap_tiles.1 = (f32[24,128,128]{2,1,0:T(8,128)}, bf16[24,128,128]{2,1,0:T(8,128)(2,1)}, f32[24,128,128]{2,1,0:T(8,128)}, f32[24,128,128]{2,1,0:T(8,128)}, f32[2...) custom-call(f32[2]{0:T(128)S(1)} %power_subtract_fusion.corrections, ...), custom_call_target="tpu_custom_call" | custom-call | flops 44000002048 | bytes 40000000 | tf_op jit(solution)/shard_map/soap_tiles/pallas_call | solution.py:1318
  (189 shorter events, 17.0 us)
Async XLA Ops:
  7.2 113.4 %all-gather.2.cloned.1.call-start = ((), (), s32[]{:S(2)}) async-start(), calls=%async_computation | async-start | bytes 7077888 | tf_op jit(solution)/shard_map/all_gather | solution.py:1377
  12.6 1.7 collective-permute-start
  15.2 6.4 %collective-permute-start.1 = (f32[7,32,128]{2,1,0:T(8,128)S(1)}, f32[7,32,128]{2,1,0:T(8,128)S(1)}, u32[]{:S(2)}, u32[]{:S(2)}) collective-permute-start(f32[7,32,128]{2,1,0:T(8,128)S(1)} %add.53), channel_id=1, source_target_pairs={{0,8},{4,12},{8,0},{12,4},{16,24},{20,28},{24,16},{28,20},{1,9},{5... | collective-permute-start | bytes 344072 | tf_op jit(solution)/shard_map/ppermute | solution.py:121
  18.1 7.4 %collective-permute-start.2 = (f32[7,32,128]{2,1,0:T(8,128)S(1)}, f32[7,32,128]{2,1,0:T(8,128)S(1)}, u32[]{:S(2)}, u32[]{:S(2)}) collective-permute-start(f32[7,32,128]{2,1,0:T(8,128)S(1)} %add.53), channel_id=1, source_target_pairs={{0,16},{4,20},{8,24},{12,28},{16,0},{20,4},{24,8},{28,12},{1,17},{... | collective-permute-start | bytes 344072 | tf_op jit(solution)/shard_map/ppermute | solution.py:121
  19.6 5.9 %collective-permute-start.3 = (f32[7,32,128]{2,1,0:T(8,128)S(1)}, f32[7,32,128]{2,1,0:T(8,128)S(1)}, u32[]{:S(2)}, u32[]{:S(2)}) collective-permute-start(f32[7,32,128]{2,1,0:T(8,128)S(1)} %add.53), channel_id=1, source_target_pairs={{0,24},{4,28},{8,16},{12,20},{16,8},{20,12},{24,0},{28,4},{1,25},{... | collective-permute-start | bytes 344072 | tf_op jit(solution)/shard_map/ppermute | solution.py:121
  25.5 1.4 collective-permute-start.4
  28.8 4.2 %collective-permute-start.5 = (f32[640,128]{1,0:T(8,128)S(1)}, f32[640,128]{1,0:T(8,128)S(1)}, u32[]{:S(2)}, u32[]{:S(2)}) collective-permute-start(f32[640,128]{1,0:T(8,128)S(1)} %get-tuple-element.115), channel_id=1, source_target_pairs={{0,4},{4,0},{8,12},{12,8},{16,20},{20,16},{24,28},{28,24},{1,5},{5... | collective-permute-start | bytes 983048 | tf_op jit(solution)/shard_map/ppermute | solution.py:121
  33.1 6.6 %collective-permute-start.6 = (f32[160,128]{1,0:T(8,128)S(1)}, f32[160,128]{1,0:T(8,128)S(1)}, u32[]{:S(2)}, u32[]{:S(2)}) collective-permute-start(f32[160,128]{1,0:T(8,128)S(1)} %get-tuple-element.196), channel_id=1, source_target_pairs={{0,8},{4,12},{8,0},{12,4},{16,24},{20,28},{24,16},{28,20},{1,9},{5... | collective-permute-start | bytes 245768 | tf_op jit(solution)/shard_map/ppermute | solution.py:121
  34.4 12.9 %collective-permute-start.10 = (bf16[512,128]{1,0:T(8,128)(2,1)S(1)}, bf16[512,128]{1,0:T(8,128)(2,1)S(1)}, u32[]{:S(2)}, u32[]{:S(2)}) collective-permute-start(bf16[512,128]{1,0:T(8,128)(2,1)S(1)} %get-tuple-element.124.refs_0_), channel_id=1, source_target_pairs={{0,2},{1,3},{2,0},{3,1},{4,6},{5,7},{6,4},{7,5},{8,10},{9,11},{10,... | collective-permute-start | bytes 393224 | tf_op jit(solution)/shard_map/ppermute | solution.py:121
  37.0 10.3 %collective-permute-start.11 = (bf16[512,128]{1,0:T(8,128)(2,1)S(1)}, bf16[512,128]{1,0:T(8,128)(2,1)S(1)}, u32[]{:S(2)}, u32[]{:S(2)}) collective-permute-start(bf16[512,128]{1,0:T(8,128)(2,1)S(1)} %get-tuple-element.124.refs_0_), channel_id=1, source_target_pairs={{0,3},{1,2},{2,1},{3,0},{4,7},{5,6},{6,5},{7,4},{8,11},{9,10},{10,... | collective-permute-start | bytes 393224 | tf_op jit(solution)/shard_map/ppermute | solution.py:121
  38.3 9.4 %collective-permute-start.9 = (bf16[512,128]{1,0:T(8,128)(2,1)S(1)}, bf16[512,128]{1,0:T(8,128)(2,1)S(1)}, u32[]{:S(2)}, u32[]{:S(2)}) collective-permute-start(bf16[512,128]{1,0:T(8,128)(2,1)S(1)} %get-tuple-element.124.refs_0_), channel_id=1, source_target_pairs={{0,1},{1,0},{2,3},{3,2},{4,5},{5,4},{6,7},{7,6},{8,9},{9,8},{10,11... | collective-permute-start | bytes 393224 | tf_op jit(solution)/shard_map/ppermute | solution.py:121
  38.5 8.2 %collective-permute-start.7 = (f32[160,128]{1,0:T(8,128)S(1)}, f32[160,128]{1,0:T(8,128)S(1)}, u32[]{:S(2)}, u32[]{:S(2)}) collective-permute-start(f32[160,128]{1,0:T(8,128)S(1)} %get-tuple-element.195), channel_id=1, source_target_pairs={{0,16},{4,20},{8,24},{12,28},{16,0},{20,4},{24,8},{28,12},{1,17},{... | collective-permute-start | bytes 245768 | tf_op jit(solution)/shard_map/ppermute | solution.py:121
  39.6 7.5 %collective-permute-start.8 = (f32[160,128]{1,0:T(8,128)S(1)}, f32[160,128]{1,0:T(8,128)S(1)}, u32[]{:S(2)}, u32[]{:S(2)}) collective-permute-start(f32[160,128]{1,0:T(8,128)S(1)} %get-tuple-element.194), channel_id=1, source_target_pairs={{0,24},{4,28},{8,16},{12,20},{16,8},{20,12},{24,0},{28,4},{1,25},{... | collective-permute-start | bytes 245768 | tf_op jit(solution)/shard_map/ppermute | solution.py:121
  47.8 30.2 %copy-start.10 = (f32[1025,32]{0,1:T(8,128)S(1)}, f32[1025,32]{0,1:T(8,128)}, u32[]{:S(2)}) copy-start(f32[1025,32]{0,1:T(8,128)} %param.48) | copy-start | bytes 393604
  47.8 30.2 %copy-start.13 = (f32[32,1024]{1,0:T(8,128)S(1)}, f32[32,1024]{1,0:T(8,128)}, u32[]{:S(2)}) copy-start(f32[32,1024]{1,0:T(8,128)} %refs_7_.1) | copy-start | bytes 393220
  47.8 30.2 %copy-start.20 = (f32[5,1024]{1,0:T(8,128)S(1)}, f32[5,1024]{1,0:T(8,128)}, u32[]{:S(2)}) copy-start(f32[5,1024]{1,0:T(8,128)} %refs_13_.1) | copy-start | bytes 61444
  47.8 5.6 %collective-permute-start.15 = (f32[160,128]{1,0:T(8,128)S(1)}, f32[160,128]{1,0:T(8,128)S(1)}, u32[]{:S(2)}, u32[]{:S(2)}) collective-permute-start(f32[160,128]{1,0:T(8,128)S(1)} %add_add_fusion.1.refs_0_), channel_id=1, source_target_pairs={{0,1},{1,0},{2,3},{3,2},{4,5},{5,4},{6,7},{7,6},{8,9},{9,8},{10,11... | collective-permute-start | bytes 245768 | tf_op jit(solution)/shard_map/ppermute | solution.py:121
  50.0 6.3 %collective-permute-start.16 = (f32[160,128]{1,0:T(8,128)S(1)}, f32[160,128]{1,0:T(8,128)S(1)}, u32[]{:S(2)}, u32[]{:S(2)}) collective-permute-start(f32[160,128]{1,0:T(8,128)S(1)} %add_add_fusion.1.refs_0_), channel_id=1, source_target_pairs={{0,2},{1,3},{2,0},{3,1},{4,6},{5,7},{6,4},{7,5},{8,10},{9,11},{10,... | collective-permute-start | bytes 245768 | tf_op jit(solution)/shard_map/ppermute | solution.py:121
  52.0 7.3 %collective-permute-start.17 = (f32[160,128]{1,0:T(8,128)S(1)}, f32[160,128]{1,0:T(8,128)S(1)}, u32[]{:S(2)}, u32[]{:S(2)}) collective-permute-start(f32[160,128]{1,0:T(8,128)S(1)} %add_add_fusion.1.refs_0_), channel_id=1, source_target_pairs={{0,3},{1,2},{2,1},{3,0},{4,7},{5,6},{6,5},{7,4},{8,11},{9,10},{10,... | collective-permute-start | bytes 245768 | tf_op jit(solution)/shard_map/ppermute | solution.py:121
  59.4 16.2 %collective-permute-start.19 = (bf16[608,128]{1,0:T(8,128)(2,1)S(1)}, bf16[608,128]{1,0:T(8,128)(2,1)S(1)}, u32[]{:S(2)}, u32[]{:S(2)}) collective-permute-start(bf16[608,128]{1,0:T(8,128)(2,1)S(1)} %pack_segments.1.refs_8_), channel_id=1, source_target_pairs={{0,8},{4,12},{8,0},{12,4},{16,24},{20,28},{24,16},{28,20},{1,9},{5... | collective-permute-start | bytes 466952 | tf_op jit(solution)/shard_map/ppermute | solution.py:121
  60.4 15.7 %collective-permute-start.21 = (bf16[608,128]{1,0:T(8,128)(2,1)S(1)}, bf16[608,128]{1,0:T(8,128)(2,1)S(1)}, u32[]{:S(2)}, u32[]{:S(2)}) collective-permute-start(bf16[608,128]{1,0:T(8,128)(2,1)S(1)} %pack_segments.1.refs_8_), channel_id=1, source_target_pairs={{0,16},{4,20},{8,24},{12,28},{16,0},{20,4},{24,8},{28,12},{1,17},{... | collective-permute-start | bytes 466952 | tf_op jit(solution)/shard_map/ppermute | solution.py:121
  61.8 14.4 %collective-permute-start.23 = (bf16[608,128]{1,0:T(8,128)(2,1)S(1)}, bf16[608,128]{1,0:T(8,128)(2,1)S(1)}, u32[]{:S(2)}, u32[]{:S(2)}) collective-permute-start(bf16[608,128]{1,0:T(8,128)(2,1)S(1)} %pack_segments.1.refs_8_), channel_id=1, source_target_pairs={{0,24},{4,28},{8,16},{12,20},{16,8},{20,12},{24,0},{28,4},{1,25},{... | collective-permute-start | bytes 466952 | tf_op jit(solution)/shard_map/ppermute | solution.py:121
  62.9 6.4 %collective-permute-start.12 = (bf16[512,128]{1,0:T(8,128)(2,1)S(1)}, bf16[512,128]{1,0:T(8,128)(2,1)S(1)}, u32[]{:S(2)}, u32[]{:S(2)}) collective-permute-start(bf16[512,128]{1,0:T(8,128)(2,1)S(1)} %get-tuple-element.128.refs_4_), channel_id=1, source_target_pairs={{0,1},{1,0},{2,3},{3,2},{4,5},{5,4},{6,7},{7,6},{8,9},{9,8},{10,11... | collective-permute-start | bytes 393224 | tf_op jit(solution)/shard_map/ppermute | solution.py:121
  64.8 10.1 %collective-permute-start.13 = (bf16[512,128]{1,0:T(8,128)(2,1)S(1)}, bf16[512,128]{1,0:T(8,128)(2,1)S(1)}, u32[]{:S(2)}, u32[]{:S(2)}) collective-permute-start(bf16[512,128]{1,0:T(8,128)(2,1)S(1)} %get-tuple-element.128.refs_4_), channel_id=1, source_target_pairs={{0,2},{1,3},{2,0},{3,1},{4,6},{5,7},{6,4},{7,5},{8,10},{9,11},{10,... | collective-permute-start | bytes 393224 | tf_op jit(solution)/shard_map/ppermute | solution.py:121
  70.0 7.7 %collective-permute-start.14 = (bf16[512,128]{1,0:T(8,128)(2,1)S(1)}, bf16[512,128]{1,0:T(8,128)(2,1)}, u32[]{:S(2)}, u32[]{:S(2)}) collective-permute-start(bf16[512,128]{1,0:T(8,128)(2,1)S(1)} %get-tuple-element.128.refs_4_), channel_id=1, source_target_pairs={{0,3},{1,2},{2,1},{3,0},{4,7},{5,6},{6,5},{7,4},{8,11},{9,10},{10,... | collective-permute-start | bytes 393224 | tf_op jit(solution)/shard_map/ppermute | solution.py:121
  75.6 2.1 %collective-permute-start.18 = (bf16[608,128]{1,0:T(8,128)(2,1)S(1)}, bf16[608,128]{1,0:T(8,128)(2,1)S(1)}, u32[]{:S(2)}, u32[]{:S(2)}) collective-permute-start(bf16[608,128]{1,0:T(8,128)(2,1)S(1)} %pack_segments.1.refs_8_), channel_id=1, source_target_pairs={{0,4},{4,0},{8,12},{12,8},{16,20},{20,16},{24,28},{28,24},{1,5},{5... | collective-permute-start | bytes 466952 | tf_op jit(solution)/shard_map/ppermute | solution.py:121
  75.6 2.1 %collective-permute-start.20 = (bf16[608,128]{1,0:T(8,128)(2,1)S(1)}, bf16[608,128]{1,0:T(8,128)(2,1)S(1)}, u32[]{:S(2)}, u32[]{:S(2)}) collective-permute-start(bf16[608,128]{1,0:T(8,128)(2,1)S(1)} %collective-permute-done.19.refs_10_), channel_id=1, source_target_pairs={{0,4},{4,0},{8,12},{12,8},{16,20},{20,16},{24,28},{28,24},{1,5},{5... | collective-permute-start | bytes 466952 | tf_op jit(solution)/shard_map/ppermute | solution.py:121
  76.1 1.6 collective-permute-start.22
  76.2 1.8 collective-permute-start.24
  93.2 5.1 %collective-permute-start.25 = (f32[104,1024]{1,0:T(8,128)S(1)}, f32[104,1024]{1,0:T(8,128)S(1)}, u32[]{:S(2)}, u32[]{:S(2)}) collective-permute-start(f32[104,1024]{1,0:T(8,128)S(1)} %get-tuple-element.135), channel_id=1, source_target_pairs={{0,4},{4,0},{8,12},{12,8},{16,20},{20,16},{24,28},{28,24},{1,5},{5... | collective-permute-start | bytes 1277960 | tf_op jit(solution)/shard_map/ppermute | solution.py:121
  98.5 7.7 %collective-permute-start.26 = (f32[56,1024]{1,0:T(8,128)S(1)}, f32[56,1024]{1,0:T(8,128)S(1)}, u32[]{:S(2)}, u32[]{:S(2)}) collective-permute-start(f32[56,1024]{1,0:T(8,128)S(1)} %slice.38), channel_id=1, source_target_pairs={{0,8},{4,12},{8,0},{12,4},{16,24},{20,28},{24,16},{28,20},{1,9},{5... | collective-permute-start | bytes 688136 | tf_op jit(solution)/shard_map/ppermute | solution.py:121
  99.2 7.8 %collective-permute-start.28 = (f32[48,1024]{1,0:T(8,128)S(1)}, f32[48,1024]{1,0:T(8,128)S(1)}, u32[]{:S(2)}, u32[]{:S(2)}) collective-permute-start(f32[48,1024]{1,0:T(8,128)S(1)} %slice.39), channel_id=1, source_target_pairs={{0,16},{4,20},{8,24},{12,28},{16,0},{20,4},{24,8},{28,12},{1,17},{... | collective-permute-start | bytes 589832 | tf_op jit(solution)/shard_map/ppermute | solution.py:121
  106.2 14.5 %copy-start.26 = (s32[192]{0:T(256)S(1)}, s32[192]{0:T(256)}, u32[]{:S(2)}) copy-start(s32[192]{0:T(256)} %owner.3) | copy-start | bytes 2308
  106.2 14.5 %copy-start.39 = (bf16[32,1024]{1,0:T(8,128)(2,1)S(1)}, bf16[32,1024]{1,0:T(8,128)(2,1)}, u32[]{:S(2)}) copy-start(bf16[32,1024]{1,0:T(8,128)(2,1)} %get-tuple-element.138.normed) | copy-start | bytes 196612
  106.2 6.9 %collective-permute-start.27 = (f32[56,1024]{1,0:T(8,128)S(1)}, f32[56,1024]{1,0:T(8,128)S(1)}, u32[]{:S(2)}, u32[]{:S(2)}) collective-permute-start(f32[56,1024]{1,0:T(8,128)S(1)} %slice_add_fusion.1), channel_id=1, source_target_pairs={{0,16},{4,20},{8,24},{12,28},{16,0},{20,4},{24,8},{28,12},{1,17},{... | collective-permute-start | bytes 688136 | tf_op jit(solution)/shard_map/ppermute | solution.py:121
  107.0 6.2 %collective-permute-start.29 = (f32[48,1024]{1,0:T(8,128)S(1)}, f32[48,1024]{1,0:T(8,128)S(1)}, u32[]{:S(2)}, u32[]{:S(2)}) collective-permute-start(f32[48,1024]{1,0:T(8,128)S(1)} %slice_add_fusion), channel_id=1, source_target_pairs={{0,8},{4,12},{8,0},{12,4},{16,24},{20,28},{24,16},{28,20},{1,9},{5... | collective-permute-start | bytes 589832 | tf_op jit(solution)/shard_map/ppermute | solution.py:121
  108.5 4.8 %collective-permute-start.31 = (f32[32,256]{1,0:T(8,128)S(1)}, f32[32,256]{1,0:T(8,128)S(1)}, u32[]{:S(2)}, u32[]{:S(2)}) collective-permute-start(f32[32,256]{1,0:T(8,128)S(1)} %broadcast_select_fusion), channel_id=1, source_target_pairs={{0,4},{4,0},{8,12},{12,8},{16,20},{20,16},{24,28},{28,24},{1,5},{5... | collective-permute-start | bytes 98312 | tf_op jit(solution)/shard_map/ppermute | solution.py:121
  113.3 7.4 %collective-permute-start.30 = (f32[104,1024]{1,0:T(8,128)S(1)}, f32[104,1024]{1,0:T(8,128)S(1)}, u32[]{:S(2)}, u32[]{:S(2)}) collective-permute-start(f32[104,1024]{1,0:T(8,128)S(1)} %pad_maximum_fusion.mine), channel_id=1, source_target_pairs={{0,4},{4,0},{8,12},{12,8},{16,20},{20,16},{24,28},{28,24},{1,5},{5... | collective-permute-start | bytes 1277960 | tf_op jit(solution)/shard_map/ppermute | solution.py:121
  113.4 4.2 %collective-permute-start.32 = (f32[32,256]{1,0:T(8,128)S(1)}, f32[32,256]{1,0:T(8,128)S(1)}, u32[]{:S(2)}, u32[]{:S(2)}) collective-permute-start(f32[32,256]{1,0:T(8,128)S(1)} %select_add_fusion), channel_id=1, source_target_pairs={{0,8},{4,12},{8,0},{12,4},{16,24},{20,28},{24,16},{28,20},{1,9},{5... | collective-permute-start | bytes 98312 | tf_op jit(solution)/shard_map/ppermute | solution.py:121
  114.8 3.9 %collective-permute-start.33 = (f32[32,256]{1,0:T(8,128)S(1)}, f32[32,256]{1,0:T(8,128)S(1)}, u32[]{:S(2)}, u32[]{:S(2)}) collective-permute-start(f32[32,256]{1,0:T(8,128)S(1)} %select_add_fusion), channel_id=1, source_target_pairs={{0,16},{4,20},{8,24},{12,28},{16,0},{20,4},{24,8},{28,12},{1,17},{... | collective-permute-start | bytes 98312 | tf_op jit(solution)/shard_map/ppermute | solution.py:121
  115.7 4.8 %collective-permute-start.34 = (f32[32,256]{1,0:T(8,128)S(1)}, f32[32,256]{1,0:T(8,128)S(1)}, u32[]{:S(2)}, u32[]{:S(2)}) collective-permute-start(f32[32,256]{1,0:T(8,128)S(1)} %select_add_fusion), channel_id=1, source_target_pairs={{0,24},{4,28},{8,16},{12,20},{16,8},{20,12},{24,0},{28,4},{1,25},{... | collective-permute-start | bytes 98312 | tf_op jit(solution)/shard_map/ppermute | solution.py:121
  120.5 18.7 %collective-permute-start.35 = (f32[32,256]{1,0:T(8,128)S(1)}, f32[32,256]{1,0:T(8,128)S(1)}, u32[]{:S(2)}, u32[]{:S(2)}) collective-permute-start(f32[32,256]{1,0:T(8,128)S(1)} %add_add_fusion.2.mine), channel_id=1, source_target_pairs={{0,4},{4,0},{8,12},{12,8},{16,20},{20,16},{24,28},{28,24},{1,5},{5... | collective-permute-start | bytes 98312 | tf_op jit(solution)/shard_map/ppermute | solution.py:121
  139.9 15.6 %collective-permute-start.36 = (f32[24,1024]{1,0:T(8,128)S(1)}, f32[24,1024]{1,0:T(8,128)S(1)}, u32[]{:S(2)}, u32[]{:S(2)}) collective-permute-start(f32[24,1024]{1,0:T(8,128)S(1)} %get-tuple-element.151), channel_id=1, source_target_pairs={{0,1},{1,0},{2,3},{3,2},{4,5},{5,4},{6,7},{7,6},{8,9},{9,8},{10,11... | collective-permute-start | bytes 294920 | tf_op jit(solution)/shard_map/ppermute | solution.py:121
  141.9 13.6 %collective-permute-start.37 = (f32[24,1024]{1,0:T(8,128)S(1)}, f32[24,1024]{1,0:T(8,128)S(1)}, u32[]{:S(2)}, u32[]{:S(2)}) collective-permute-start(f32[24,1024]{1,0:T(8,128)S(1)} %get-tuple-element.151), channel_id=1, source_target_pairs={{0,2},{1,3},{2,0},{3,1},{4,6},{5,7},{6,4},{7,5},{8,10},{9,11},{10,... | collective-permute-start | bytes 294920 | tf_op jit(solution)/shard_map/ppermute | solution.py:121
  145.0 10.5 %collective-permute-start.38 = (f32[24,1024]{1,0:T(8,128)S(1)}, f32[24,1024]{1,0:T(8,128)S(1)}, u32[]{:S(2)}, u32[]{:S(2)}) collective-permute-start(f32[24,1024]{1,0:T(8,128)S(1)} %get-tuple-element.151), channel_id=1, source_target_pairs={{0,3},{1,2},{2,1},{3,0},{4,7},{5,6},{6,5},{7,4},{8,11},{9,10},{10,... | collective-permute-start | bytes 294920 | tf_op jit(solution)/shard_map/ppermute | solution.py:121
  155.5 1.4 collective-permute-start.39
  155.6 1.4 collective-permute-start.40
  156.1 1.3 collective-permute-start.41
  (51 other events, 428.5 us)
Sparse Core Ops, SparseCore 0:
  25.6 56.0 all-gather.1
